TPU v7x, 32 devices: a whole 2x2x4 slice. The times are simulated.
32 devices in a mesh: dp: 4 (over y, core), wide: 8 (over z, x).
Axes of the slice: x: 2, y: 2, z: 4, core: 2. Of those that a mesh axis runs over, the one named last changes fastest.
Arguments:
- tokens: bfloat16 [32768, 768], P(('dp', 'wide')), may hold values from -6 to 6
- segments: int32 [32768], P(('dp', 'wide')), may hold values from 0 to 15, as said below
- counts: int32 [32], P(('dp', 'wide')), may hold values from 256 to 1024, as said below
- out_grad: bfloat16 [32768, 768], P(('dp', 'wide')), may hold values from -6 to 6
- attn_param: float32 [2363136], P(('dp', 'wide')), may hold values from -2.5 to 2.5
- attn_moment: float32 [2363136], P(('dp', 'wide')), may hold values from -0.03125 to 0.03125
- attn_square: float32 [2363136], P(('dp', 'wide')), may hold values from 1e-09 to 1e-07
- attn_shadow: float32 [2363136], P(('dp', 'wide')), may hold values from -0.75 to 0.75
- ffn_param: float32 [4723968], P(('dp', 'wide')), may hold values from -1.5 to 1.5
- ffn_moment: float32 [4723968], P(('dp', 'wide')), may hold values from -0.03125 to 0.03125
- ffn_square: float32 [4723968], P(('dp', 'wide')), may hold values from 1e-09 to 1e-07
- ffn_shadow: float32 [4723968], P(('dp', 'wide')), may hold values from -0.75 to 0.75
Outputs:
- activations: bfloat16 [32768, 768], P(('dp', 'wide'))
- pooled: float32 [512, 768], P(('dp', 'wide'))
- token_grad: bfloat16 [32768, 768], P(('dp', 'wide'))
- attn_grad: float32 [2363136], P(('dp', 'wide'))
- ffn_grad: float32 [4723968], P(('dp', 'wide'))
- attn_change: float32 [2363136], P(('dp', 'wide'))
- ffn_change: float32 [4723968], P(('dp', 'wide'))
- moment_attn: float32 [2363136], P(('dp', 'wide'))
- moment_ffn: float32 [4723968], P(('dp', 'wide'))
- square_attn: float32 [2363136], P(('dp', 'wide'))
- square_ffn: float32 [4723968], P(('dp', 'wide'))
- drift_attn: float32 [2363136], P(('dp', 'wide'))
- drift_ffn: float32 [4723968], P(('dp', 'wide'))
Inputs may be any that keep to these rules, and one draw needn't show every extreme that they name: `counts`: true tokens of each row of 1024 positions; the later positions of the row are padding. `segments`: starts at 0 and never falls within each row of 1024 positions; a run of one number is 64 to 256 positions long, the last run of a row possibly shorter.
All inputs are finite; a program needn't handle non-finite values.
Results may differ from a plain program's by a relative error of at most 0.012.
The roundings to bfloat16 on the way count: a program that leaves them out, or rounds other values in their place, can miss the bound.
Values may be sent and summed in bfloat16 or wider, within the bound.
No kernel may reach another device: no remote copies, remote signals or barrier semaphores. Data moves between devices by JAX's collectives and lax.ppermute only.
A program may use at most 256 MiB of HBM per device.

v0:
```python
import jax
import jax.numpy as jnp
from jax import lax
from jax.sharding import PartitionSpec as P

D = 768
FF = 3072
HEAD = 64
HEADS = 12
ROW = 1024
STEP = 10
CROPS = 16


HIGHEST = lax.Precision.HIGHEST
NORM_EPSILON = 1e-12
NEGATIVE = -1e30
MOMENT_DECAY = 0.9
SQUARE_DECAY = 0.999
LEARN_RATE = 0.001
WEIGHT_DECAY = 0.01
ADAM_EPSILON = 1e-08
SHADOW_RATE = 0.9995


def split_attn(flat):
    matrix_size = D * D
    w_query = flat[0:matrix_size].reshape(D, D)
    w_key = flat[matrix_size : 2 * matrix_size].reshape(D, D)
    w_value = flat[2 * matrix_size : 3 * matrix_size].reshape(D, D)
    w_out = flat[3 * matrix_size : 4 * matrix_size].reshape(D, D)
    offset = 4 * matrix_size
    b_query = flat[offset : offset + D]
    b_value = flat[offset + D : offset + 2 * D]
    b_out = flat[offset + 2 * D : offset + 3 * D]
    gain_one = flat[offset + 3 * D : offset + 4 * D]
    shift_one = flat[offset + 4 * D : offset + 5 * D]
    return (w_query, w_key, w_value, w_out, b_query, b_value, b_out, gain_one, shift_one)


def split_ffn(flat):
    matrix_size = D * FF
    w_up = flat[0:matrix_size].reshape(D, FF)
    w_down = flat[matrix_size : 2 * matrix_size].reshape(FF, D)
    offset = 2 * matrix_size
    b_up = flat[offset : offset + FF]
    b_down = flat[offset + FF : offset + FF + D]
    gain_two = flat[offset + FF + D : offset + FF + 2 * D]
    shift_two = flat[offset + FF + 2 * D : offset + FF + 3 * D]
    return (w_up, w_down, b_up, b_down, gain_two, shift_two)


def layer_norm(resid, gain, shift):
    centred = resid - jnp.mean(resid, axis=-1, keepdims=True)
    spread = jnp.mean(centred * centred, axis=-1, keepdims=True)
    return centred * lax.rsqrt(spread + NORM_EPSILON) * gain + shift


def gelu_exact(inputs):
    return jax.nn.gelu(inputs, approximate=False)


def contract_rows(left, right):
    return lax.dot_general(
        left, right, (((0,), (0,)), ((), ())), preferred_element_type=jnp.float32
    )


def contract_cols(left, right):
    return lax.dot_general(
        left, right, (((1,), (1,)), ((), ())), preferred_element_type=jnp.float32
    )


def flatten_grads(pieces, length_all):
    joined = jnp.concatenate([piece.reshape(-1) for piece in pieces])
    return jnp.concatenate([joined, jnp.zeros((length_all - joined.shape[0],), jnp.float32)])


def add_rows(whole, addend):
    return whole + addend


def block_parts(queries, keys, values, segments, is_valid, block_index, block_rows):
    block_start = block_index * block_rows
    row_start = block_start // ROW * ROW
    query_blk = lax.dynamic_slice_in_dim(queries, block_start, block_rows, 0).reshape(
        block_rows, HEADS, HEAD
    )
    key_row = keys.reshape(ROW, HEADS, HEAD)
    value_row = values.reshape(ROW, HEADS, HEAD)
    scores = jnp.einsum(
        "qhe,khe->hqk", query_blk, key_row, preferred_element_type=jnp.float32
    ) * HEAD ** (-0.5)
    query_seg = lax.dynamic_slice_in_dim(segments, block_start, block_rows, 0)
    query_pos = block_start + jnp.arange(block_rows, dtype=jnp.int32)
    key_pos = row_start + jnp.arange(ROW, dtype=jnp.int32)
    allowed = (query_seg[:, None] == segments[None, :]) & is_valid[None, :] | (
        query_pos[:, None] == key_pos[None, :]
    )
    scores = jnp.where(allowed[None], scores, NEGATIVE)
    return (block_start, row_start, query_blk, key_row, value_row, scores)


def adam_update(param, gradient, moment, square, shadow):
    step_float = float(STEP)
    moment_next = MOMENT_DECAY * moment + (1.0 - MOMENT_DECAY) * gradient
    square_next = SQUARE_DECAY * square + (1.0 - SQUARE_DECAY) * gradient * gradient
    moment_hat = moment_next / (1.0 - MOMENT_DECAY**step_float)
    square_hat = square_next / (1.0 - SQUARE_DECAY**step_float)
    change = -LEARN_RATE * (
        moment_hat / (jnp.sqrt(square_hat) + ADAM_EPSILON) + WEIGHT_DECAY * param
    )
    updated = param + change
    drift = (1.0 - SHADOW_RATE) * (updated - shadow)
    return (change, moment_next, square_next, drift)


def on_device(
    tokens,
    segments,
    counts,
    out_grad,
    attn_param,
    attn_moment,
    attn_square,
    attn_shadow,
    ffn_param,
    ffn_moment,
    ffn_square,
    ffn_shadow,
):
    row_count = counts.shape[0]
    tok_rows = row_count * ROW
    block_rows = min(512, ROW)
    block_count = tok_rows // block_rows
    scale = HEAD ** (-0.5)
    position = jnp.arange(ROW, dtype=jnp.int32)
    is_valid = (position[None, :] < counts[:, None]).reshape(tok_rows)
    token_total = lax.psum(jnp.sum(counts).astype(jnp.float32), ("dp", "wide"))
    attn_whole = lax.all_gather(attn_param.astype(jnp.bfloat16), ("dp", "wide"), axis=0, tiled=True)
    w_query, w_key, w_value, w_out, b_query, b_value, b_out, gain_one, shift_one = split_attn(
        attn_whole
    )
    queries = (
        jnp.dot(tokens, w_query, preferred_element_type=jnp.float32) + b_query.astype(jnp.float32)
    ).astype(jnp.bfloat16)
    keys = jnp.dot(tokens, w_key, preferred_element_type=jnp.float32).astype(jnp.bfloat16)
    values = (
        jnp.dot(tokens, w_value, preferred_element_type=jnp.float32) + b_value.astype(jnp.float32)
    ).astype(jnp.bfloat16)

    def attend_forward(block_index):
        parts = block_parts(queries, keys, values, segments, is_valid, block_index, block_rows)
        value_row = parts[4]
        scores = parts[5]
        top_score = jnp.max(scores, axis=-1, keepdims=True)
        shifted = jnp.exp(scores - top_score)
        denominator = jnp.sum(shifted, axis=-1, keepdims=True)
        att_prob = (shifted / denominator).astype(jnp.bfloat16)
        mixed_blk = jnp.einsum(
            "hqk,khe->qhe", att_prob, value_row, preferred_element_type=jnp.float32
        )
        return (
            mixed_blk.reshape(block_rows, D).astype(jnp.bfloat16),
            (top_score + jnp.log(denominator))[..., 0],
        )

    mixed_blocks, log_totals = lax.map(attend_forward, jnp.arange(block_count, dtype=jnp.int32))
    mixed = mixed_blocks.reshape(tok_rows, D)
    attn_proj = jnp.dot(mixed, w_out, preferred_element_type=jnp.float32) + b_out.astype(
        jnp.float32
    )
    resid_one = tokens.astype(jnp.float32) + attn_proj
    hidden_one, norm_one_pull = jax.vjp(
        layer_norm, resid_one, gain_one.astype(jnp.float32), shift_one.astype(jnp.float32)
    )
    ffn_whole = lax.all_gather(ffn_param.astype(jnp.bfloat16), ("dp", "wide"), axis=0, tiled=True)
    w_up, w_down, b_up, b_down, gain_two, shift_two = split_ffn(ffn_whole)
    hidden_low = hidden_one.astype(jnp.bfloat16)
    pre_act = jnp.dot(hidden_low, w_up, preferred_element_type=jnp.float32) + b_up.astype(
        jnp.float32
    )
    activated = gelu_exact(pre_act).astype(jnp.bfloat16)
    ffn_proj = jnp.dot(activated, w_down, preferred_element_type=jnp.float32) + b_down.astype(
        jnp.float32
    )
    resid_two = hidden_one + ffn_proj
    final_out, norm_two_pull = jax.vjp(
        layer_norm, resid_two, gain_two.astype(jnp.float32), shift_two.astype(jnp.float32)
    )
    one_hot = (
        (
            segments.reshape(row_count, ROW)[:, :, None]
            == jnp.arange(CROPS, dtype=jnp.int32)[None, None, :]
        )
        & is_valid.reshape(row_count, ROW)[:, :, None]
    ).astype(jnp.float32)
    crop_sums = jnp.einsum(
        "rpc,rpd->rcd", one_hot, final_out.reshape(row_count, ROW, D), precision=HIGHEST
    )
    crop_sizes = jnp.sum(one_hot, axis=1)
    pooled = (crop_sums / jnp.maximum(crop_sizes, 1.0)[:, :, None]).reshape(row_count * CROPS, D)
    cotangent = out_grad.astype(jnp.float32) * is_valid[:, None].astype(jnp.float32)
    grad_resid_two, grad_gain_two, grad_shift_two = norm_two_pull(cotangent)
    grad_ffn_out = grad_resid_two.astype(jnp.bfloat16)
    ffn_back = lax.all_gather(ffn_param.astype(jnp.bfloat16), ("dp", "wide"), axis=0, tiled=True)
    w_up_back, w_down_back = split_ffn(ffn_back)[:2]
    grad_w_down = contract_rows(activated, grad_ffn_out)
    grad_b_down = jnp.sum(grad_ffn_out.astype(jnp.float32), axis=0)
    grad_act = contract_cols(grad_ffn_out, w_down_back)
    gelu_pull = jax.vjp(gelu_exact, pre_act)[1]
    grad_pre = gelu_pull(grad_act)[0].astype(jnp.bfloat16)
    grad_w_up = contract_rows(hidden_low, grad_pre)
    grad_b_up = jnp.sum(grad_pre.astype(jnp.float32), axis=0)
    grad_hidden = grad_resid_two + contract_cols(grad_pre, w_up_back)
    ffn_full = flatten_grads(
        [grad_w_up, grad_w_down, grad_b_up, grad_b_down, grad_gain_two, grad_shift_two],
        ffn_whole.shape[0],
    )
    ffn_summed = lax.psum_scatter(ffn_full, ("dp", "wide"), scatter_dimension=0, tiled=True)
    grad_resid_one, grad_gain_one, grad_shift_one = norm_one_pull(grad_hidden)
    grad_attn_out = grad_resid_one.astype(jnp.bfloat16)
    attn_back = lax.all_gather(attn_param.astype(jnp.bfloat16), ("dp", "wide"), axis=0, tiled=True)
    w_query_back, w_key_back, w_value_back, w_out_back = split_attn(attn_back)[:4]
    grad_w_out = contract_rows(mixed, grad_attn_out)
    grad_b_out = jnp.sum(grad_attn_out.astype(jnp.float32), axis=0)
    grad_mixed = contract_cols(grad_attn_out, w_out_back).astype(jnp.bfloat16)

    def attend_backward(carried, block_inputs):
        grad_keys_acc, grad_values_acc = carried
        block_index, log_total = block_inputs
        block_start, row_start, query_blk, key_row, value_row, scores = block_parts(
            queries, keys, values, segments, is_valid, block_index, block_rows
        )
        att_prob = jnp.exp(scores - log_total[..., None])
        grad_blk = lax.dynamic_slice_in_dim(grad_mixed, block_start, block_rows, 0).reshape(
            block_rows, HEADS, HEAD
        )
        grad_prob = jnp.einsum(
            "qhe,khe->hqk", grad_blk, value_row, preferred_element_type=jnp.float32
        )
        grad_scores = (
            att_prob * (grad_prob - jnp.sum(att_prob * grad_prob, axis=-1, keepdims=True))
        ).astype(jnp.bfloat16)
        grad_query = (
            jnp.einsum("hqk,khe->qhe", grad_scores, key_row, preferred_element_type=jnp.float32)
            * scale
        )
        key_part = (
            jnp.einsum("hqk,qhe->khe", grad_scores, query_blk, preferred_element_type=jnp.float32)
            * scale
        )
        value_part = jnp.einsum(
            "hqk,qhe->khe",
            att_prob.astype(jnp.bfloat16),
            grad_blk,
            preferred_element_type=jnp.float32,
        )
        grad_keys_acc = add_rows(grad_keys_acc, key_part.reshape(ROW, D))
        grad_values_acc = add_rows(grad_values_acc, value_part.reshape(ROW, D))
        return ((grad_keys_acc, grad_values_acc), grad_query.reshape(block_rows, D))

    zero_rows = jnp.zeros((tok_rows, D), jnp.float32)
    sums_back, query_blocks = lax.scan(
        attend_backward,
        (zero_rows, zero_rows),
        (jnp.arange(block_count, dtype=jnp.int32), log_totals),
    )
    grad_queries = query_blocks.reshape(tok_rows, D).astype(jnp.bfloat16)
    grad_keys = sums_back[0].astype(jnp.bfloat16)
    grad_values = sums_back[1].astype(jnp.bfloat16)
    grad_w_query = contract_rows(tokens, grad_queries)
    grad_w_key = contract_rows(tokens, grad_keys)
    grad_w_value = contract_rows(tokens, grad_values)
    grad_b_query = jnp.sum(grad_queries.astype(jnp.float32), axis=0)
    grad_b_value = jnp.sum(grad_values.astype(jnp.float32), axis=0)
    token_grad = (
        grad_resid_one
        + contract_cols(grad_queries, w_query_back)
        + contract_cols(grad_keys, w_key_back)
        + contract_cols(grad_values, w_value_back)
    ).astype(jnp.bfloat16)
    attn_full = flatten_grads(
        [
            grad_w_query,
            grad_w_key,
            grad_w_value,
            grad_w_out,
            grad_b_query,
            grad_b_value,
            grad_b_out,
            grad_gain_one,
            grad_shift_one,
        ],
        attn_whole.shape[0],
    )
    attn_summed = lax.psum_scatter(attn_full, ("dp", "wide"), scatter_dimension=0, tiled=True)
    attn_grad = attn_summed / token_total
    ffn_grad = ffn_summed / token_total
    attn_change, moment_attn, square_attn, drift_attn = adam_update(
        attn_param, attn_grad, attn_moment, attn_square, attn_shadow
    )
    ffn_change, moment_ffn, square_ffn, drift_ffn = adam_update(
        ffn_param, ffn_grad, ffn_moment, ffn_square, ffn_shadow
    )
    return (
        final_out.astype(jnp.bfloat16),
        pooled,
        token_grad,
        attn_grad,
        ffn_grad,
        attn_change,
        ffn_change,
        moment_attn,
        moment_ffn,
        square_attn,
        square_ffn,
        drift_attn,
        drift_ffn,
    )


def solution(mesh):
    placed = (
        P(("dp", "wide"), None),
        P(("dp", "wide")),
        P(("dp", "wide")),
        P(("dp", "wide"), None),
        P(("dp", "wide")),
        P(("dp", "wide")),
        P(("dp", "wide")),
        P(("dp", "wide")),
        P(("dp", "wide")),
        P(("dp", "wide")),
        P(("dp", "wide")),
        P(("dp", "wide")),
    )
    return jax.shard_map(
        on_device,
        mesh=mesh,
        in_specs=placed,
        out_specs=(
            P(("dp", "wide"), None),
            P(("dp", "wide"), None),
            P(("dp", "wide"), None),
            P(("dp", "wide")),
            P(("dp", "wide")),
            P(("dp", "wide")),
            P(("dp", "wide")),
            P(("dp", "wide")),
            P(("dp", "wide")),
            P(("dp", "wide")),
            P(("dp", "wide")),
            P(("dp", "wide")),
            P(("dp", "wide")),
        ),
        check_vma=False,
    )
```

profile of v0, /device:TPU:8, one launch (start us, length us, event | category | flops | bytes accessed | tf_op | source)
XLA Modules:
  0.0 1241.3 jit_solution(15052786570108801963)
XLA Ops:
  30.4 245.7 %all-reduce.11.cloned.1.call-done = (bf16[2363136]{0:T(1024)(128)(2,1)}, bf16[4723968]{0:T(1024)(128)(2,1)}) async-done(((bf16[2363136]{0:T(1024)(128)(2,1)}, bf16[4723968]{0:T(1024)(128)(2,1)}), (bf16[2363136]{0:T(1024)(128)(2,1)}, bf16[4723968]{0:T(1024)(128)(2,1)})) %all-reduce.11.cloned.1.call-update) | async-done | bytes 14174224
  277.4 8.5 fusion.60
  290.8 9.2 slice.117
  317.0 80.7 %while.32 = (s32[]{:T(128)}, bf16[2,512,768]{2,1,0:T(8,128)(2,1)}, f32[2,12,512]{2,1,0:T(8,128)S(1)}, s32[2]{0:T(128)S(1)}, s32[1024]{0:T(1024)S(1)}, /*index=5*...) while((s32[]{:T(128)}, bf16[2,512,768]{2,1,0:T(8,128)(2,1)}, ...), condition=%wide.region_3.4_spmd.clone, body=%wide.region_0.3_spmd.clone.sunk | while | flops 1688596992 | bytes 187941296 | solution.py:169
  321.3 10.7 fusion.131
  331.9 12.3 fusion.132
  347.3 9.0 fusion.133
  361.4 10.7 fusion.131
  372.1 12.3 fusion.132
  387.5 9.0 fusion.133
  404.9 8.4 reshape.587
  413.3 37.2 %multiply_convert_fusion.1 = (bf16[1024,3072]{1,0:T(8,128)(2,1)S(1)}, f32[1024,3072]{1,0:T(8,128)}, f32[1024,3072]{1,0:T(8,128)}) fusion(f32[3072]{0:T(1024)S(1)} %copy-done.63, bf16[768,3072]{1,0:T(8,128)(2,1)} %reshape.587, f32[1024,768]{0,1:T(8,128)S(1)} %copy-done.18, f32[768]{0:T(1024)S(1)} %copy-done.64, f32[768]{0:T(1024)S(1)} %copy-done.57, ...), kind=kOutput, calls=%fused_computation.42 | convolution fusion | flops 5043388416 | bytes 39348224 | tf_op jit(solution)/shard_map/dot_general | solution.py:181
  450.6 10.3 fusion.63
  468.2 18.1 %convert_reduce_fusion = (f32[3072]{0:T(1024)}, bf16[1024,3072]{1,0:T(8,128)(2,1)}) fusion(f32[1024,3072]{1,0:T(8,128)} %get-tuple-element.519, bf16[1024,768]{0,1:T(8,128)(2,1)S(1)} %get-tuple-element.513, bf16[3072,768]{1,0:T(8,128)(2,1)} %slice.117, f32[1024,3072]{1,0:T(8,128)} %get-tuple-element.545, f32[3072]{0:T(1024)S(1)} %copy-done.63), kind=kOutput, calls=%fused_computation.40 | convolution fusion | flops 4885312512 | bytes 37773312 | tf_op jit(solution)/shard_map/dot_general | solution.py:70
  486.3 12.1 multiply_reduce_fusion.2
  498.3 7.9 convolution_bitcast_fusion
  514.9 183.4 %while.33 = (s32[]{:T(128)}, f32[1024,768]{0,1:T(8,128)}, f32[1024,768]{0,1:T(8,128)}, bf16[2,512,768]{2,1,0:T(8,128)(2,1)}, s32[2]{0:T(128)S(1)}, /*index=5*/bf...) while((s32[]{:T(128)}, f32[1024,768]{0,1:T(8,128)}, ...), condition=%wide.region_15.16_spmd.clone, body=%wide.region_13.15_spmd.clone.sunk | while | flops 4127715840 | bytes 298779232 | solution.py:265
  521.3 10.1 fusion.144
  531.4 13.1 %fusion.145 = f32[12,64,1024]{2,1,0:T(8,128)} fusion(bf16[512,12,64]{0,2,1:T(8,128)(2,1)S(1)} %bitcast.149, f32[12,512,1024]{2,1,0:T(8,128)} %fusion.144, f32[12,512]{1,0:T(8,128)S(1)} %dynamic-slice_bitcast_fusion.2, pred[512,1024]{1,0:T(8,128)(4,1)S(1)} %compare_or_fusion.5), kind=kOutput, calls=%fused_computation.22.clone.1 | convolution fusion | flops 830472192 | bytes 29646848 | tf_op jit(solution)/shard_map/while/body/eval_jaxpr/hqk,qhe->khe/dot_general | solution.py:254
  544.5 18.1 %multiply_reduce_fusion.8 = (f32[12,512]{1,0:T(8,128)S(1)}, f32[12,512,1024]{2,1,0:T(8,128)}) fusion(f32[12,512,1024]{2,1,0:T(8,128)} %fusion.144, f32[12,512]{1,0:T(8,128)S(1)} %dynamic-slice_bitcast_fusion.2, pred[512,1024]{1,0:T(8,128)(4,1)S(1)} %compare_or_fusion.5, bf16[512,12,64]{0,2,1:T(8,128)(2,1)} %bitcast.148, ...), kind=kOutput, calls=%fused_computation.19.clone.1 | convolution fusion | flops 836757504 | bytes 53264384 | tf_op jit(solution)/shard_map/while/body/eval_jaxpr/qhe,khe->hqk/dot_general | solution.py:240
  562.6 21.2 %multiply_convert_fusion.3 = bf16[12,512,1024]{2,1,0:T(8,128)(2,1)} fusion(f32[12,512,1024]{2,1,0:T(8,128)} %get-tuple-element.692, f32[12,512,1024]{2,1,0:T(8,128)} %fusion.144, f32[12,512]{1,0:T(8,128)S(1)} %get-tuple-element.693, f32[12,512]{1,0:T(8,128)S(1)} %dynamic-slice_bitcast_fusion.2, pred[512,1024]{1,0:T(8,128)(4,1)S(1)} %compare_or_fusion.5), kind=kLoop, calls=%fused_computation.18.clone.1 | loop fusion | flops 37748736 | bytes 63488000 | tf_op jit(solution)/shard_map/while/body/eval_jaxpr/convert_element_type | solution.py:245
  583.8 8.5 convolution_multiply_fusion.5
  612.6 10.1 fusion.144
  622.8 13.1 %fusion.145 = f32[12,64,1024]{2,1,0:T(8,128)} fusion(bf16[512,12,64]{0,2,1:T(8,128)(2,1)S(1)} %bitcast.149, f32[12,512,1024]{2,1,0:T(8,128)} %fusion.144, f32[12,512]{1,0:T(8,128)S(1)} %dynamic-slice_bitcast_fusion.2, pred[512,1024]{1,0:T(8,128)(4,1)S(1)} %compare_or_fusion.5), kind=kOutput, calls=%fused_computation.22.clone.1 | convolution fusion | flops 830472192 | bytes 29646848 | tf_op jit(solution)/shard_map/while/body/eval_jaxpr/hqk,qhe->khe/dot_general | solution.py:254
  635.8 18.1 %multiply_reduce_fusion.8 = (f32[12,512]{1,0:T(8,128)S(1)}, f32[12,512,1024]{2,1,0:T(8,128)}) fusion(f32[12,512,1024]{2,1,0:T(8,128)} %fusion.144, f32[12,512]{1,0:T(8,128)S(1)} %dynamic-slice_bitcast_fusion.2, pred[512,1024]{1,0:T(8,128)(4,1)S(1)} %compare_or_fusion.5, bf16[512,12,64]{0,2,1:T(8,128)(2,1)} %bitcast.148, ...), kind=kOutput, calls=%fused_computation.19.clone.1 | convolution fusion | flops 836757504 | bytes 53264384 | tf_op jit(solution)/shard_map/while/body/eval_jaxpr/qhe,khe->hqk/dot_general | solution.py:240
  653.9 21.2 %multiply_convert_fusion.3 = bf16[12,512,1024]{2,1,0:T(8,128)(2,1)} fusion(f32[12,512,1024]{2,1,0:T(8,128)} %get-tuple-element.692, f32[12,512,1024]{2,1,0:T(8,128)} %fusion.144, f32[12,512]{1,0:T(8,128)S(1)} %get-tuple-element.693, f32[12,512]{1,0:T(8,128)S(1)} %dynamic-slice_bitcast_fusion.2, pred[512,1024]{1,0:T(8,128)(4,1)S(1)} %compare_or_fusion.5), kind=kLoop, calls=%fused_computation.18.clone.1 | loop fusion | flops 37748736 | bytes 63488000 | tf_op jit(solution)/shard_map/while/body/eval_jaxpr/convert_element_type | solution.py:245
  675.1 8.5 convolution_multiply_fusion.5
  705.5 10.4 fusion.67
  755.5 10.8 reshape.593
  768.2 9.2 constant_dynamic-update-slice_fusion.5
  792.4 42.1 %psum.7 = f32[]{:T(128)} all-reduce(f32[]{:T(128)S(6)} %convert_element_type.195), channel_id=1, replica_groups=mesh['dp'=4,'wide'=8] {'dp','wide'}, use_global_device_ids=true, to_apply=%region_22.23 | all-reduce | flops 1 | bytes 8 | tf_op jit(solution)/shard_map/psum | solution.py:140
  851.7 375.3 %all-reduce.9.cloned.1.call-done = (f32[2363136]{0:T(1024)}, f32[4723968]{0:T(1024)}) async-done(((f32[2363136]{0:T(1024)}, f32[4723968]{0:T(1024)}), (f32[2363136]{0:T(1024)}, f32[4723968]{0:T(1024)})) %all-reduce.9.cloned.1.call-update) | async-done | bytes 28348432
  (304 shorter events, 210.5 us)
Async XLA Ops:
  7.2 268.9 %all-reduce.11.cloned.1.call-start = ((), (), s32[]{:S(2)}) async-start(), calls=%async_computation.1 | async-start | bytes 28352512
  25.2 1201.8 %all-reduce.9.cloned.1.call-start = ((), (), s32[]{:S(2)}) async-start(), calls=%async_computation | async-start | bytes 56705024
  302.6 11.7 copy-start.25
  317.0 80.7 %copy-start.66 = (f32[768]{0:T(1024)S(1)}, f32[768]{0:T(1024)}, u32[]{:S(2)}) copy-start(f32[768]{0:T(1024)} %get-tuple-element.554) | copy-start | bytes 9220
  331.9 15.4 %copy-start = (f32[12,512,1024]{2,1,0:T(8,128)S(1)}, f32[12,512,1024]{2,1,0:T(8,128)}, u32[]{:S(2)}) copy-start(f32[12,512,1024]{2,1,0:T(8,128)} %get-tuple-element.678) | copy-start | bytes 75497472 | tf_op jit(solution)/shard_map/while
  372.1 15.4 %copy-start = (f32[12,512,1024]{2,1,0:T(8,128)S(1)}, f32[12,512,1024]{2,1,0:T(8,128)}, u32[]{:S(2)}) copy-start(f32[12,512,1024]{2,1,0:T(8,128)} %get-tuple-element.678) | copy-start | bytes 75497472 | tf_op jit(solution)/shard_map/while
  413.3 37.2 %copy-start.19 = (f32[1024,768]{0,1:T(8,128)S(1)}, f32[1024,768]{0,1:T(8,128)}, u32[]{:S(2)}) copy-start(f32[1024,768]{0,1:T(8,128)} %copy-done.17) | copy-start | bytes 9437188
  413.3 37.2 %copy-start.65 = (f32[768]{0:T(1024)S(1)}, f32[768]{0:T(1024)}, u32[]{:S(2)}) copy-start(f32[768]{0:T(1024)} %get-tuple-element.527) | copy-start | bytes 9220
  450.5 10.3 copy-start.71
  450.5 10.3 copy-start.15
  450.6 10.3 copy-start.44
  450.6 10.3 copy-start.48
  460.9 25.4 %copy-start.11 = (f32[1024,768]{0,1:T(8,128)}, f32[1024,768]{0,1:T(8,128)S(1)}, u32[]{:S(2)}) copy-start(f32[1024,768]{0,1:T(8,128)S(1)} %get-tuple-element.547) | copy-start | bytes 9437188
  460.9 25.4 %copy-start.46 = (f32[1024]{0:T(1024)}, f32[1024]{0:T(1024)S(1)}, u32[]{:S(2)}) copy-start(f32[1024]{0:T(1024)S(1)} %broadcast_multiply_fusion) | copy-start | bytes 12292
  462.6 23.6 %copy-start.53 = (f32[1024]{0:T(1024)}, f32[1024]{0:T(1024)S(1)}, u32[]{:S(2)}) copy-start(f32[1024]{0:T(1024)S(1)} %get-tuple-element.542) | copy-start | bytes 12292
  468.2 18.1 %copy-start.31 = (bf16[1024,768]{0,1:T(8,128)(2,1)}, bf16[1024,768]{0,1:T(8,128)(2,1)S(1)}, u32[]{:S(2)}) copy-start(bf16[1024,768]{0,1:T(8,128)(2,1)S(1)} %get-tuple-element.513) | copy-start | bytes 4718596
  486.2 12.1 copy-start.20
  486.3 12.1 copy-start.70
  521.2 10.2 copy-start.10
  612.6 10.2 copy-start.10
  701.1 14.8 %slice-start.3 = ((s8[9437184]{0:T(1024)(128)(4,1)}), s8[4194304]{0:T(1024)(128)(4,1)S(1)}, s32[]{:S(2)}) async-start(s8[9437184]{0:T(1024)(128)(4,1)} %bitcast.155), calls=%async_computation.5 | async-start | bytes 8388608
  705.5 10.4 slice-start.4
  705.5 10.4 slice-start.5
  768.1 9.3 copy-start.22
  768.1 13.3 %slice-start = ((s8[9437184]{0:T(1024)(128)(4,1)}), s8[4194304]{0:T(1024)(128)(4,1)S(1)}, s32[]{:S(2)}) async-start(s8[9437184]{0:T(1024)(128)(4,1)} %bitcast.150), calls=%async_computation.2 | async-start | bytes 8388608
  768.2 13.3 %slice-start.1 = ((s8[9437184]{0:T(1024)(128)(4,1)}), s8[4194304]{0:T(1024)(128)(4,1)S(1)}, s32[]{:S(2)}) async-start(s8[9437184]{0:T(1024)(128)(4,1)} %bitcast.150), calls=%async_computation.3 | async-start | bytes 8388608
  781.5 9.6 copy-start.58
  845.7 381.3 %copy-start.33 = (f32[73848]{0:T(1024)S(1)}, f32[73848]{0:T(1024)}, u32[]{:S(2)}) copy-start(f32[73848]{0:T(1024)} %param.20) | copy-start | bytes 886180
  851.7 378.6 %copy-start.27 = (f32[147624]{0:T(1024)S(1)}, f32[147624]{0:T(1024)}, u32[]{:S(2)}) copy-start(f32[147624]{0:T(1024)} %param.24) | copy-start | bytes 1771492
  851.7 378.6 %copy-start.39 = (f32[147624]{0:T(1024)S(1)}, f32[147624]{0:T(1024)}, u32[]{:S(2)}) copy-start(f32[147624]{0:T(1024)} %param.27) | copy-start | bytes 1771492
  851.7 378.6 %copy-start.40 = (f32[147624]{0:T(1024)S(1)}, f32[147624]{0:T(1024)}, u32[]{:S(2)}) copy-start(f32[147624]{0:T(1024)} %param.25) | copy-start | bytes 1771492
  851.7 378.6 %copy-start.41 = (f32[147624]{0:T(1024)S(1)}, f32[147624]{0:T(1024)}, u32[]{:S(2)}) copy-start(f32[147624]{0:T(1024)} %param.26) | copy-start | bytes 1771492
  (55 other events, 234.0 us)
Sparse Core Ops, SparseCore 0:
  25.3 250.7 all-reduce.10
  792.6 434.4 all-reduce.8
where the time goes:
time: 1250 us; the launch traced here: 1240 us
  waiting for transfers between devices  621 us (50%)
  matrix products  292 us (23%)
  local copies, waits for them, and re-layouts  163 us (13%)
  other arithmetic  103 us (8%)
  blocking collectives  42.1 us (3%)
  between operations  15.7 us (1%)
    unnamed x4, waiting for transfers between devices  621 us
    unnamed x164, local copies, waits for them, and re-layouts  60.7 us
    convert_element_type x2, other arithmetic, attend_backward(): grad_scores = (att_prob * (grad_prob - jnp.sum(att_prob * grad_prob, axis...  42.4 us
    psum x1, blocking collectives, on_device(): token_total = lax.psum(jnp.sum(counts).astype(jnp.float32), ('dp', 'wide'))  42.1 us
    dot_general x4, matrix products, block_parts(): jnp.einsum('qhe,khe->hqk', query_blk, key_row, preferred_element_type=jnp...  41.6 us
    dot_general x6, matrix products, contract_cols(): lax.dot_general(left, right, (((1,), (1,)), ((), ())), preferred_element_...  40.3 us
    dot_general x1, matrix products, on_device(): jnp.dot(hidden_low, w_up, preferred_element_type=jnp.float32)  37.2 us
    dot_general x2, matrix products, attend_backward(): jnp.einsum('qhe,khe->hqk', grad_blk, value_row, preferred_element_type=jn...  36.2 us
  transfers between devices with their start and end apart: 2, of which 2 were waited for; matrix products, arithmetic and copies ran while one was open for 2% of the time, Pallas kernels for 0%

commit v1 on v0

v1 whole, which is shorter than its diff:
```python
import functools

import jax
import jax.numpy as jnp
from jax import lax
from jax.experimental import pallas as pl
from jax.experimental.pallas import tpu as pltpu
from jax.sharding import PartitionSpec as P

D = 768
FF = 3072
HEAD = 64
HEADS = 12
ROW = 1024
STEP = 10
CROPS = 16

NORM_EPSILON = 1e-12
NEGATIVE = -1e30
MOMENT_DECAY = 0.9
SQUARE_DECAY = 0.999
LEARN_RATE = 0.001
WEIGHT_DECAY = 0.01
ADAM_EPSILON = 1e-08
SHADOW_RATE = 0.9995
SCALE = HEAD ** (-0.5)

AXES = ("dp", "wide")
BF = jnp.bfloat16
F32 = jnp.float32
UP_CHUNKS = FF // D
ATTN_ROWS = 4 * D
FFN_ROWS = 2 * FF
ATTN_TAIL = 5 * D
FFN_TAIL = FF + 3 * D
VEC_ROWS = 16
COUNT_ROW = 12
MIB = 1 << 20


def dot(left, right, left_dim, right_dim):
    return lax.dot_general(
        left, right, (((left_dim,), (right_dim,)), ((), ())), preferred_element_type=F32
    )


class Places:
    def __init__(self, mesh):
        self.dp, self.wide = mesh.shape["dp"], mesh.shape["wide"]
        self.count = self.dp * self.wide
        self.size = {"c": 2, "y": self.dp // 2}
        self.size["x"] = self.size["y"]
        self.size["z"] = self.wide // self.size["x"]

    def staged(self):
        exact = self.dp % 2 == 0 and self.wide % self.size["x"] == 0
        return exact and ATTN_ROWS % (32 * self.count) == 0

    def index(self, y, c, z, x):
        return (y * 2 + c) * self.wide + z * self.size["x"] + x

    def rotation(self, axis, step):
        pairs = []
        extent = self.size
        for y in range(extent["y"]):
            for c in range(2):
                for z in range(extent["z"]):
                    for x in range(extent["x"]):
                        at = {"y": y, "c": c, "z": z, "x": x}
                        to = dict(at)
                        to[axis] = (at[axis] + step) % extent[axis]
                        pairs.append((self.index(**at), self.index(**to)))
        return pairs

    def send(self, array, axis, step):
        return lax.ppermute(array, AXES, self.rotation(axis, step))

    def here(self):
        outer, inner = lax.axis_index("dp"), lax.axis_index("wide")
        extent = self.size["x"]
        return {"y": outer // 2, "c": outer % 2, "z": inner // extent, "x": inner % extent}


def pick(array, index, axis):
    return lax.dynamic_index_in_dim(array, index, axis, keepdims=False)


def small_sum(places, array):
    for axis in ("c", "z", "x", "y"):
        total = array
        for step in range(1, places.size[axis]):
            total = total + places.send(array, axis, step)
        array = total
    return array


def gather_pieces(places, own):
    extent = places.size
    rows = own.shape[0]
    half_rows = rows // 2
    blocks = [own] + [places.send(own, "z", k) for k in range(1, extent["z"])]
    pieces = []
    for half, (first, second) in enumerate((("x", "y"), ("y", "x"))):
        held = jnp.concatenate([b[half * half_rows : (half + 1) * half_rows] for b in blocks], 0)
        where = [{"z": k} for k in range(extent["z"])]
        near, near_where = [held], list(where)
        for k in range(1, extent[first]):
            near.append(places.send(held, first, k))
            near_where += [dict(w, **{first: k}) for w in where]
        near = jnp.concatenate(near, 0)
        groups = [(near, near_where)]
        for k in range(1, extent[second]):
            groups.append((places.send(near, second, k), [dict(w, **{second: k}) for w in near_where]))
        groups += [(places.send(g, "c", 1), [dict(w, c=1) for w in ws]) for g, ws in groups]
        pieces += [
            (g, [(w.get("z", 0), w.get("x", 0), w.get("y", 0), w.get("c", 0), half) for w in ws])
            for g, ws in groups
        ]
    return pieces


def owner_index(places, here, offsets):
    extent = places.size
    dz, dx, dy, dc, _ = offsets
    return places.index(
        lax.rem(here["y"] + (extent["y"] - dy), extent["y"]),
        lax.rem(here["c"] + (2 - dc), 2),
        lax.rem(here["z"] + (extent["z"] - dz), extent["z"]),
        lax.rem(here["x"] + (extent["x"] - dx), extent["x"]),
    )


def assemble(places, me, pieces, rows, cut, place):
    def kernel(me_ref, *refs):
        out, sem = refs[-2:]
        here = {"y": me_ref[0], "c": me_ref[1], "z": me_ref[2], "x": me_ref[3]}
        for (_, offsets), ref in zip(pieces, refs):
            step = ref.shape[0] // len(offsets)
            part_rows = step // cut
            for i, off in enumerate(offsets):
                owner = owner_index(places, here, off)
                for part in range(cut):
                    start = pl.multiple_of(place(owner, off[4], part), 16)
                    pltpu.make_async_copy(
                        ref.at[pl.ds(i * step + part * part_rows, part_rows)],
                        out.at[pl.ds(start, part_rows)],
                        sem,
                    ).start()
        pltpu.make_async_copy(out, out, sem).wait()

    return pl.pallas_call(
        kernel,
        in_specs=[pl.BlockSpec(memory_space=pltpu.SMEM)]
        + [pl.BlockSpec(memory_space=pl.ANY)] * len(pieces),
        out_specs=pl.BlockSpec(memory_space=pl.ANY),
        out_shape=jax.ShapeDtypeStruct((rows, D), BF),
        scratch_shapes=[pltpu.SemaphoreType.DMA],
        name="assemble",
    )(me, *[p for p, _ in pieces])


def scatter_sum(places, here, parts):
    extent = places.size

    def add(own, arrived):
        total = own.astype(F32)
        for a in arrived:
            total = total + a.astype(F32)
        return total

    def reduce_axis(array, axis, dim):
        arrived = [
            places.send(pick(array, lax.rem(here[axis] + k, extent[axis]), dim), axis, k)
            for k in range(1, extent[axis])
        ]
        return add(pick(array, here[axis], dim), arrived)

    summed = jnp.stack([reduce_axis(p, "c", 0).astype(BF) for p in parts])
    half_rows = summed.shape[3] // 2
    first = summed[:, :, :, :half_rows]
    second = summed[:, :, :, half_rows:]
    first = reduce_axis(first, "y", 0).astype(BF)
    second = reduce_axis(second, "x", 2).astype(BF)
    first = reduce_axis(first, "x", 1).astype(BF)
    second = reduce_axis(second, "y", 0).astype(BF)
    return reduce_axis(jnp.concatenate([first, second], 1), "z", 0)


def to_rows(places, me, flat, rows, tail):
    count = places.count
    block = rows // count * D
    slack = tail // count
    before = lax.ppermute(flat[-tail:], AXES, [(i, i + 1) for i in range(count - 1)])
    joined = jnp.concatenate([before, flat])
    return lax.dynamic_slice_in_dim(joined, tail - me * slack, block).reshape(rows // count, D)


def to_flat(places, me, block, vectors, tail):
    count = places.count
    slack = tail // count
    after = lax.ppermute(block[: tail // D], AXES, [(i + 1, i) for i in range(count - 1)])
    after = jnp.where(me == count - 1, vectors, after)
    joined = jnp.concatenate([block, after], 0).reshape(-1)
    return lax.dynamic_slice_in_dim(joined, me * slack, block.size + slack)


def project_kernel(tokens, weights, vec, query, key, value):
    held = tokens[...]
    query[...] = (dot(held, weights[0], 1, 0) + vec[0:1]).astype(BF)
    key[...] = dot(held, weights[1], 1, 0).astype(BF)
    value[...] = (dot(held, weights[2], 1, 0) + vec[1:2]).astype(BF)


def project(tokens, weights, vec):
    rows = tokens.shape[0]
    step = 256
    tile = pl.BlockSpec((step, D), lambda i: (i, 0))
    return pl.pallas_call(
        project_kernel,
        grid=(rows // step,),
        in_specs=[
            tile,
            pl.BlockSpec((3, D, D), lambda i: (0, 0, 0), pipeline_mode=pl.Buffered(1)),
            pl.BlockSpec((VEC_ROWS, D), lambda i: (0, 0)),
        ],
        out_specs=[tile] * 3,
        out_shape=[jax.ShapeDtypeStruct((rows, D), BF)] * 3,
        compiler_params=pltpu.CompilerParams(vmem_limit_bytes=40 * MIB),
        name="project",
    )(tokens, weights, vec)


QUERY_BLOCK = 256
QUERY_BLOCKS = ROW // QUERY_BLOCK


def window(block):
    low = max(0, block - 1) * QUERY_BLOCK
    return low, min(QUERY_BLOCKS, block + 2) * QUERY_BLOCK


def fill_bias(bias, seg_column, seg_row, count):
    for block in range(QUERY_BLOCKS):
        low, high = window(block)
        at = slice(block * QUERY_BLOCK, (block + 1) * QUERY_BLOCK)
        shape = (high - low, QUERY_BLOCK)
        key_pos = low + lax.broadcasted_iota(jnp.int32, shape, 0)
        query_pos = block * QUERY_BLOCK + lax.broadcasted_iota(jnp.int32, shape, 1)
        same = seg_column[low:high, 0:1] == seg_row[0:1, at]
        allowed = (same & (key_pos < count)) | (key_pos == query_pos)
        bias[0 : high - low, at] = jnp.where(allowed, 0.0, NEGATIVE).astype(F32)


def one_head(transposed):
    zero = jnp.zeros((HEAD, transposed.shape[1]), transposed.dtype)
    return (
        jnp.concatenate([transposed[:HEAD], zero], 0),
        jnp.concatenate([zero, transposed[HEAD:]], 0),
    )


def attend_kernel(count, seg_column, seg_row, query, key, value, mixed, log_total, bias):
    @pl.when(pl.program_id(0) == 0)
    def _():
        fill_bias(bias, seg_column, seg_row, count[0])

    value_t = value[...].T
    query_t = one_head((query[...] * jnp.asarray(SCALE, BF)).T)
    for block in range(QUERY_BLOCKS):
        low, high = window(block)
        at = slice(block * QUERY_BLOCK, (block + 1) * QUERY_BLOCK)
        parts = []
        for h in range(2):
            scores = dot(key[low:high, :], query_t[h][:, at], 1, 0) + bias[0 : high - low, at]
            top = jnp.max(scores, axis=0, keepdims=True)
            shifted = jnp.exp(scores - top)
            total = jnp.sum(shifted, axis=0, keepdims=True)
            part = dot(value_t[h * HEAD : (h + 1) * HEAD, low:high], shifted.astype(BF), 1, 0)
            parts.append(part * (1.0 / total))
            log_total[0, h : h + 1, at] = top + jnp.log(total)
        mixed[at, :] = jnp.concatenate(parts, 0).T.astype(BF)


def attend_specs():
    return [
        pl.BlockSpec(memory_space=pltpu.SMEM),
        pl.BlockSpec((ROW, 1), lambda h: (0, 0)),
        pl.BlockSpec((1, ROW), lambda h: (0, 0)),
    ]


def attend(query, key, value, segments, count):
    pair = pl.BlockSpec((ROW, 2 * HEAD), lambda h: (0, h))
    return pl.pallas_call(
        attend_kernel,
        grid=(HEADS // 2,),
        in_specs=attend_specs() + [pair] * 3,
        out_specs=[pair, pl.BlockSpec((1, 8, ROW), lambda h: (h, 0, 0))],
        out_shape=[
            jax.ShapeDtypeStruct((ROW, D), BF),
            jax.ShapeDtypeStruct((HEADS // 2, 8, ROW), F32),
        ],
        scratch_shapes=[pltpu.VMEM((3 * QUERY_BLOCK, ROW), F32)],
        compiler_params=pltpu.CompilerParams(vmem_limit_bytes=40 * MIB),
        name="attend",
    )(count, segments.reshape(ROW, 1), segments.reshape(1, ROW), query, key, value)


def attend_back_kernel(
    count, seg_column, seg_row, query, key, value, grad, log_total, grad_query, grad_key, grad_value, bias, key_sum, value_sum
):
    @pl.when(pl.program_id(0) == 0)
    def _():
        fill_bias(bias, seg_column, seg_row, count[0])

    query_t = (query[...] * jnp.asarray(SCALE, BF)).T
    key_t = key[...].T
    grad_t = grad[...].T
    query_one, grad_one = one_head(query_t), one_head(grad_t)
    key_sum[...] = jnp.zeros_like(key_sum)
    value_sum[...] = jnp.zeros_like(value_sum)
    for block in range(QUERY_BLOCKS):
        low, high = window(block)
        at = slice(block * QUERY_BLOCK, (block + 1) * QUERY_BLOCK)
        parts = []
        for h in range(2):
            rows = slice(h * HEAD, (h + 1) * HEAD)
            scores = dot(key[low:high, :], query_one[h][:, at], 1, 0) + bias[0 : high - low, at]
            probs = jnp.exp(scores - log_total[0, h : h + 1, at])
            grad_probs = dot(value[low:high, :], grad_one[h][:, at], 1, 0)
            weighted = probs * grad_probs
            total = jnp.sum(weighted, axis=0, keepdims=True)
            grad_scores = (weighted - probs * total).astype(BF)
            parts.append(dot(key_t[rows, low:high], grad_scores, 1, 0))
            key_sum[rows, low:high] += dot(query_t[rows, at], grad_scores, 1, 1)
            value_sum[rows, low:high] += dot(grad_t[rows, at], probs.astype(BF), 1, 1)
        grad_query[at, :] = (jnp.concatenate(parts, 0) * SCALE).T.astype(BF)
    grad_key[...] = key_sum[...].T.astype(BF)
    grad_value[...] = value_sum[...].T.astype(BF)


def attend_back(query, key, value, grad, log_total, segments, count):
    pair = pl.BlockSpec((ROW, 2 * HEAD), lambda h: (0, h))
    return pl.pallas_call(
        attend_back_kernel,
        grid=(HEADS // 2,),
        in_specs=attend_specs() + [pair] * 4 + [pl.BlockSpec((1, 8, ROW), lambda h: (h, 0, 0))],
        out_specs=[pair] * 3,
        out_shape=[jax.ShapeDtypeStruct((ROW, D), BF)] * 3,
        scratch_shapes=[
            pltpu.VMEM((3 * QUERY_BLOCK, ROW), F32),
            pltpu.VMEM((2 * HEAD, ROW), F32),
            pltpu.VMEM((2 * HEAD, ROW), F32),
        ],
        compiler_params=pltpu.CompilerParams(vmem_limit_bytes=48 * MIB),
        name="attend_back",
    )(count, segments.reshape(ROW, 1), segments.reshape(1, ROW), query, key, value, grad, log_total)


def normalise(resid):
    centred = resid - jnp.mean(resid, axis=-1, keepdims=True)
    spread = jnp.mean(centred * centred, axis=-1, keepdims=True)
    inverse = lax.rsqrt(spread + NORM_EPSILON)
    return centred * inverse, inverse


def normalise_back(cotangent, gain, normal, inverse):
    scaled = cotangent * gain
    mean = jnp.mean(scaled, axis=-1, keepdims=True)
    aligned = jnp.mean(scaled * normal, axis=-1, keepdims=True)
    return inverse * (scaled - mean - normal * aligned)


def column_sum(array):
    return jnp.sum(array, axis=0, keepdims=True)


MIDDLE_ROWS = 256


def middle_kernel(
    count,
    seg_row,
    mixed,
    tokens,
    out_grad,
    w_out,
    w_ffn,
    vec,
    final_low,
    hidden_low,
    activated,
    grad_pre,
    grad_ffn_out,
    grad_attn_out,
    grad_mixed,
    grad_resid,
    vec_grad,
    crop_sums,
    slope,
):
    step = pl.program_id(0)

    @pl.when(step == 0)
    def _():
        vec_grad[...] = jnp.zeros_like(vec_grad)
        crop_sums[...] = jnp.zeros_like(crop_sums)

    def row(i):
        return vec[i : i + 1]

    def note(i, value):
        vec_grad[i : i + 1] += value

    resid_one = tokens[...].astype(F32) + (dot(mixed[...], w_out[...], 1, 0) + row(2))
    normal_one, inverse_one = normalise(resid_one)
    hidden = normal_one * row(3) + row(4)
    low = hidden.astype(BF)
    hidden_low[...] = low
    total = hidden + row(9)
    for j in range(UP_CHUNKS):
        at = slice(j * D, (j + 1) * D)
        pre = dot(low, w_ffn[j], 1, 0) + row(5 + j)
        share = 0.5 + 0.5 * lax.erf(pre * (0.5**0.5))
        density = jnp.exp(-0.5 * pre * pre) * 0.3989422804014327
        slope[:, at] = share + pre * density
        act = (pre * share).astype(BF)
        activated[:, at] = act
        total = total + dot(act, w_ffn[UP_CHUNKS + j], 1, 0)
    normal_two, inverse_two = normalise(total)
    final = normal_two * row(10) + row(11)
    final_low[...] = final.astype(BF)

    first = step * MIDDLE_ROWS
    across = (CROPS, MIDDLE_ROWS)
    position = first + lax.broadcasted_iota(jnp.int32, across, 1)
    crop = lax.broadcasted_iota(jnp.int32, across, 0)
    member = ((seg_row[...] == crop) & (position < count[0])).astype(BF)
    high = final.astype(BF)
    rest = final - high.astype(F32)
    mid = rest.astype(BF)
    tiny = (rest - mid.astype(F32)).astype(BF)
    crop_sums[...] += dot(member, high, 1, 0) + (dot(member, mid, 1, 0) + dot(member, tiny, 1, 0))

    position = first + lax.broadcasted_iota(jnp.int32, (MIDDLE_ROWS, 1), 0)
    valid = (position < count[0]).astype(F32)
    cotangent = out_grad[...].astype(F32) * valid
    note(10, column_sum(cotangent * normal_two))
    note(11, column_sum(cotangent))
    grad_two = normalise_back(cotangent, row(10), normal_two, inverse_two)
    grad_out = grad_two.astype(BF)
    grad_ffn_out[...] = grad_out
    note(9, column_sum(grad_out.astype(F32)))
    grad_hidden = grad_two
    for j in range(UP_CHUNKS):
        at = slice(j * D, (j + 1) * D)
        back = (dot(grad_out, w_ffn[UP_CHUNKS + j], 1, 1) * slope[:, at]).astype(BF)
        grad_pre[:, at] = back
        note(5 + j, column_sum(back.astype(F32)))
        grad_hidden = grad_hidden + dot(back, w_ffn[j], 1, 1)
    note(3, column_sum(grad_hidden * normal_one))
    note(4, column_sum(grad_hidden))
    grad_one = normalise_back(grad_hidden, row(3), normal_one, inverse_one)
    grad_resid[...] = grad_one
    grad_proj = grad_one.astype(BF)
    grad_attn_out[...] = grad_proj
    note(2, column_sum(grad_proj.astype(F32)))
    grad_mixed[...] = dot(grad_proj, w_out[...], 1, 1).astype(BF)


def middle(count, segments, mixed, tokens, out_grad, w_out, w_ffn, vec):
    rows = tokens.shape[0]
    tile = pl.BlockSpec((MIDDLE_ROWS, D), lambda i: (i, 0))
    wide = pl.BlockSpec((MIDDLE_ROWS, FF), lambda i: (i, 0))
    small = pl.BlockSpec((VEC_ROWS, D), lambda i: (0, 0))

    def shape(width, kind):
        return jax.ShapeDtypeStruct((rows, width), kind)

    return pl.pallas_call(
        middle_kernel,
        grid=(rows // MIDDLE_ROWS,),
        in_specs=[
            pl.BlockSpec(memory_space=pltpu.SMEM),
            pl.BlockSpec((1, MIDDLE_ROWS), lambda i: (0, i)),
            tile,
            tile,
            tile,
            pl.BlockSpec((D, D), lambda i: (0, 0), pipeline_mode=pl.Buffered(1)),
            pl.BlockSpec((2 * UP_CHUNKS, D, D), lambda i: (0, 0, 0), pipeline_mode=pl.Buffered(1)),
            small,
        ],
        out_specs=[tile, tile, wide, wide, tile, tile, tile, tile, small, small],
        out_shape=[
            shape(D, BF),
            shape(D, BF),
            shape(FF, BF),
            shape(FF, BF),
            shape(D, BF),
            shape(D, BF),
            shape(D, BF),
            shape(D, F32),
            jax.ShapeDtypeStruct((VEC_ROWS, D), F32),
            jax.ShapeDtypeStruct((CROPS, D), F32),
        ],
        scratch_shapes=[pltpu.VMEM((MIDDLE_ROWS, FF), F32)],
        compiler_params=pltpu.CompilerParams(vmem_limit_bytes=56 * MIB),
        name="middle",
    )(count, segments.reshape(1, rows), mixed, tokens, out_grad, w_out, w_ffn, vec)


def adam_update(param, gradient, moment, square, shadow):
    step_float = float(STEP)
    moment_next = MOMENT_DECAY * moment + (1.0 - MOMENT_DECAY) * gradient
    square_next = SQUARE_DECAY * square + (1.0 - SQUARE_DECAY) * gradient * gradient
    moment_hat = moment_next / (1.0 - MOMENT_DECAY**step_float)
    square_hat = square_next / (1.0 - SQUARE_DECAY**step_float)
    change = -LEARN_RATE * (
        moment_hat / (jnp.sqrt(square_hat) + ADAM_EPSILON) + WEIGHT_DECAY * param
    )
    updated = param + change
    drift = (1.0 - SHADOW_RATE) * (updated - shadow)
    return (change, moment_next, square_next, drift)


def contract_rows(left, right):
    return dot(left, right, 0, 0)


def on_device(
    places,
    tokens,
    segments,
    counts,
    out_grad,
    attn_param,
    attn_moment,
    attn_square,
    attn_shadow,
    ffn_param,
    ffn_moment,
    ffn_square,
    ffn_shadow,
):
    assert counts.shape[0] == 1 and tokens.shape[0] == ROW
    number = places.count
    here = places.here()
    place_list = jnp.stack([here[a] for a in ("y", "c", "z", "x")]).astype(jnp.int32)
    me = lax.axis_index("dp") * places.wide + lax.axis_index("wide")
    staged = places.staged()
    attn_rows, ffn_rows = ATTN_ROWS // number, FFN_ROWS // number
    up_rows = ffn_rows // UP_CHUNKS
    holds_up = me < number // 2

    last = (me == number - 1).astype(F32)
    ends = jnp.concatenate([attn_param[-ATTN_TAIL:], ffn_param[-FFN_TAIL:]]) * last
    count_row = jnp.full((D,), counts[0].astype(F32), F32)
    small = jnp.concatenate(
        [ends, count_row, jnp.zeros(((VEC_ROWS - COUNT_ROW - 1) * D,), F32)]
    ).reshape(VEC_ROWS, D)
    if staged:
        small = small_sum(places, small)
    else:
        small = lax.psum(small, AXES)
    token_total = small[COUNT_ROW, 0]
    vec = small.astype(BF).astype(F32)

    if staged:
        attn_own = to_rows(places, me, attn_param, ATTN_ROWS, ATTN_TAIL).astype(BF)
        ffn_own = to_rows(places, me, ffn_param, FFN_ROWS, FFN_TAIL).astype(BF)
        by_chunk = ffn_own.reshape(up_rows, UP_CHUNKS, D).transpose(1, 0, 2).reshape(ffn_rows, D)
        ffn_own = jnp.where(holds_up, by_chunk, ffn_own)
        attn_whole = assemble(
            places,
            place_list,
            gather_pieces(places, attn_own),
            ATTN_ROWS,
            1,
            lambda owner, half, part: owner * attn_rows + half * (attn_rows // 2),
        ).reshape(4, D, D)

        def ffn_place(owner, half, part):
            chunk = half * (UP_CHUNKS // 2) + part
            return jnp.where(
                owner < number // 2,
                chunk * D + owner * up_rows,
                FF + (owner - number // 2) * ffn_rows + chunk * up_rows,
            )

        w_ffn = assemble(
            places,
            place_list,
            gather_pieces(places, ffn_own),
            FFN_ROWS,
            UP_CHUNKS // 2,
            ffn_place,
        ).reshape(2 * UP_CHUNKS, D, D)
    else:
        flat = lax.all_gather(attn_param.astype(BF), AXES, axis=0, tiled=True)
        attn_whole = flat[: ATTN_ROWS * D].reshape(4, D, D)
        flat = lax.all_gather(ffn_param.astype(BF), AXES, axis=0, tiled=True)
        w_up = flat[: FF * D].reshape(D, UP_CHUNKS, D).transpose(1, 0, 2)
        w_down = flat[FF * D : FFN_ROWS * D].reshape(UP_CHUNKS, D, D)
        w_ffn = jnp.concatenate([w_up, w_down], 0)

    query, key, value = project(tokens, attn_whole, vec)
    mixed, log_total = attend(query, key, value, segments, counts)
    (
        final_low,
        hidden_low,
        activated,
        grad_pre,
        grad_ffn_out,
        grad_attn_out,
        grad_mixed,
        grad_resid,
        vec_grad,
        crop_sums,
    ) = middle(counts, segments, mixed, tokens, out_grad, attn_whole[3], w_ffn, vec)
    is_valid = jnp.arange(ROW, dtype=jnp.int32) < counts[0]
    member = (segments[None, :] == jnp.arange(CROPS, dtype=jnp.int32)[:, None]) & is_valid[None, :]
    crop_sizes = jnp.sum(member.astype(F32), axis=1)
    pooled = crop_sums / jnp.maximum(crop_sizes, 1.0)[:, None]

    grad_w_down = contract_rows(activated, grad_ffn_out)
    grad_w_up = [
        contract_rows(hidden_low, grad_pre[:, j * D : (j + 1) * D]) for j in range(UP_CHUNKS)
    ]
    if staged:
        extent = places.size
        split = (extent["y"] // 2, 2, extent["z"], extent["x"])
        up = jnp.stack(
            [g.astype(BF).reshape(number // 2, up_rows, D) for g in grad_w_up], 1
        ).reshape(split + (ffn_rows, D))
        down = grad_w_down.astype(BF).reshape(split + (ffn_rows, D))
        ffn_parts = [up[y] for y in range(split[0])] + [down[y] for y in range(split[0])]
        ffn_block = scatter_sum(places, here, ffn_parts)
        by_row = ffn_block.reshape(UP_CHUNKS, up_rows, D).transpose(1, 0, 2).reshape(ffn_rows, D)
        ffn_block = jnp.where(holds_up, by_row, ffn_block)

    grad_w_out = contract_rows(mixed, grad_attn_out)
    grad_query, grad_key, grad_value = attend_back(
        query, key, value, grad_mixed, log_total, segments, counts
    )
    grad_w_query = contract_rows(tokens, grad_query)
    grad_w_key = contract_rows(tokens, grad_key)
    grad_w_value = contract_rows(tokens, grad_value)
    grad_b_query = jnp.sum(grad_query.astype(F32), axis=0)
    grad_b_value = jnp.sum(grad_value.astype(F32), axis=0)
    token_grad = (
        grad_resid
        + dot(grad_query, attn_whole[0], 1, 1)
        + dot(grad_key, attn_whole[1], 1, 1)
        + dot(grad_value, attn_whole[2], 1, 1)
    ).astype(BF)
    vec_grad = jnp.concatenate([jnp.stack([grad_b_query, grad_b_value]), vec_grad[2:]], 0)
    if staged:
        vec_sum = small_sum(places, vec_grad)
        mats = [grad_w_query, grad_w_key, grad_w_value, grad_w_out]
        mats = jnp.stack([m.astype(BF) for m in mats]).reshape(
            extent["y"], 2, extent["z"], extent["x"], attn_rows, D
        )
        attn_block = scatter_sum(places, here, [mats[y] for y in range(extent["y"])])
        attn_summed = to_flat(places, me, attn_block, vec_sum[:5], ATTN_TAIL)
        ffn_summed = to_flat(places, me, ffn_block, vec_sum[5:12], FFN_TAIL)
    else:
        attn_full = jnp.concatenate(
            [g.reshape(-1) for g in (grad_w_query, grad_w_key, grad_w_value, grad_w_out, vec_grad[:5])]
        )
        up = jnp.stack(grad_w_up, 1)
        ffn_full = jnp.concatenate([g.reshape(-1) for g in (up, grad_w_down, vec_grad[5:12])])
        attn_summed = lax.psum_scatter(attn_full, AXES, scatter_dimension=0, tiled=True)
        ffn_summed = lax.psum_scatter(ffn_full, AXES, scatter_dimension=0, tiled=True)
    attn_grad = attn_summed / token_total
    ffn_grad = ffn_summed / token_total
    attn_change, moment_attn, square_attn, drift_attn = adam_update(
        attn_param, attn_grad, attn_moment, attn_square, attn_shadow
    )
    ffn_change, moment_ffn, square_ffn, drift_ffn = adam_update(
        ffn_param, ffn_grad, ffn_moment, ffn_square, ffn_shadow
    )
    return (
        final_low,
        pooled,
        token_grad,
        attn_grad,
        ffn_grad,
        attn_change,
        ffn_change,
        moment_attn,
        moment_ffn,
        square_attn,
        square_ffn,
        drift_attn,
        drift_ffn,
    )


def solution(mesh):
    rows, flat = P(AXES, None), P(AXES)
    return jax.shard_map(
        functools.partial(on_device, Places(mesh)),
        mesh=mesh,
        in_specs=(rows, flat, flat, rows) + (flat,) * 8,
        out_specs=(rows, rows, rows) + (flat,) * 10,
        check_vma=False,
    )
```

time: 1250 us -> 826 us (0.66)
  Pallas kernels: 0 us -> 533 us
  waiting for transfers between devices: 621 us -> 141 us
  matrix products: 292 us -> 26.3 us
  local copies, waits for them, and re-layouts: 163 us -> 23.1 us
  other arithmetic: 103 us -> 21.7 us
  starting transfers between devices: 0.08 us -> 68.8 us
  blocking collectives: 42.1 us -> 0 us
  between operations: 15.7 us -> 2.85 us
    unnamed x4 -> x0, waiting for transfers between devices: 621 us -> none
    pallas_call x0 -> x6, Pallas kernels: none -> 533 us  [the longest x2 432 us: assemble(): pl.pallas_call(kernel, in_specs=[pl.BlockSpec(memory_space=pltpu.SMEM)] +...]
    dot_general x33 -> x12, matrix products: 292 us -> 26.3 us  [dot(): lax.dot_general(left, right, (((left_dim,), (right_dim,)), ((), ())), pre...]
    ppermute x0 -> x56, waiting for transfers between devices: none -> 141 us  [the longest x52 140 us: send(): return lax.ppermute(array, AXES, self.rotation(axis, step))]
    ppermute x0 -> x56, starting transfers between devices: none -> 68.8 us  [the longest x52 56.2 us: send(): return lax.ppermute(array, AXES, self.rotation(axis, step))]
    unnamed x164 -> x77, local copies, waits for them, and re-layouts: 60.7 us -> 8.9 us
    convert_element_type x7 -> x11, other arithmetic: 47.7 us -> 2.9 us  [the longest x1 1.15 us: on_device(): attn_own = to_rows(places, me, attn_param, ATTN_ROWS, ATTN_TAIL).astype(BF)]
    psum x1 -> x0, blocking collectives: 42.1 us -> none  [on_device(): token_total = lax.psum(jnp.sum(counts).astype(jnp.float32), ('dp', 'wide'))]
  transfers between devices with their start and end apart: 2 -> 56, of which waited for: 2 -> 24; matrix products, arithmetic and copies ran while one was open for 2% -> 6% of each run, Pallas kernels for 0% -> 21%
where the time goes in v1:
time: 826 us; the launch traced here: 817 us
  Pallas kernels  533 us (65%)
  waiting for transfers between devices  141 us (17%)
  starting transfers between devices  68.8 us (8%)
  matrix products  26.3 us (3%)
  local copies, waits for them, and re-layouts  23.1 us (3%)
  other arithmetic  21.7 us (3%)
    pallas_call x2, Pallas kernels, assemble(): pl.pallas_call(kernel, in_specs=[pl.BlockSpec(memory_space=pltpu.SMEM)] +...  432 us
    ppermute x52, waiting for transfers between devices, send(): return lax.ppermute(array, AXES, self.rotation(axis, step))  140 us
    ppermute x52, starting transfers between devices, send(): return lax.ppermute(array, AXES, self.rotation(axis, step))  56.2 us
    pallas_call x1, Pallas kernels, middle(): pl.pallas_call(middle_kernel, grid=(rows // MIDDLE_ROWS,), in_specs=[pl.B...  38.6 us
    pallas_call x1, Pallas kernels, attend_back(): pl.pallas_call(attend_back_kernel, grid=(HEADS // 2,), in_specs=attend_sp...  32.9 us
    dot_general x12, matrix products, dot(): lax.dot_general(left, right, (((left_dim,), (right_dim,)), ((), ())), pre...  26.3 us
    pallas_call x1, Pallas kernels, attend(): pl.pallas_call(attend_kernel, grid=(HEADS // 2,), in_specs=attend_specs()...  25 us
  transfers between devices with their start and end apart: 56, of which 24 were waited for; matrix products, arithmetic and copies ran while one was open for 6% of the time, Pallas kernels for 21%

profile of v1, /device:TPU:8, one launch (start us, length us, event | category | flops | bytes accessed | tf_op | source)
XLA Modules:
  0.0 817.3 jit_solution(6485444281335070309)
XLA Ops:
  1.5 3.4 collective-permute-start
  5.7 3.4 collective-permute-start.18
  11.0 2.6 collective-permute-start.2
  18.3 20.8 %collective-permute-done.1 = bf16[96,768]{1,0:T(8,128)(2,1)S(1)} collective-permute-done((bf16[96,768]{1,0:T(8,128)(2,1)S(1)}, bf16[96,768]{1,0:T(8,128)(2,1)S(1)}, u32[]{:S(2)}, u32[]{:S(2)}) %collective-permute-start.1) | collective-permute-done | bytes 147488 | tf_op jit(solution)/shard_map/ppermute | solution.py:76
  41.8 9.0 %collective-permute-done.19 = bf16[192,768]{1,0:T(8,128)(2,1)S(1)} collective-permute-done((bf16[192,768]{1,0:T(8,128)(2,1)S(1)}, bf16[192,768]{1,0:T(8,128)(2,1)S(1)}, u32[]{:S(2)}, u32[]{:S(2)}) %collective-permute-start.19) | collective-permute-done | bytes 294944 | tf_op jit(solution)/shard_map/ppermute | solution.py:76
  57.1 10.5 %collective-permute-done.26 = bf16[384,768]{1,0:T(8,128)(2,1)S(1)} collective-permute-done((bf16[384,768]{1,0:T(8,128)(2,1)S(1)}, bf16[384,768]{1,0:T(8,128)(2,1)S(1)}, u32[]{:S(2)}, u32[]{:S(2)}) %collective-permute-start.26) | collective-permute-done | bytes 589856 | tf_op jit(solution)/shard_map/ppermute | solution.py:76
  68.5 2.5 collective-permute-start.27
  73.8 3.4 collective-permute-start.14
  83.8 20.2 %collective-permute-done.16 = f32[16,768]{1,0:T(8,128)S(1)} collective-permute-done((f32[16,768]{1,0:T(8,128)S(1)}, f32[16,768]{1,0:T(8,128)S(1)}, u32[]{:S(2)}, u32[]{:S(2)}) %collective-permute-start.16) | collective-permute-done | bytes 49184 | tf_op jit(solution)/shard_map/ppermute | solution.py:76
  109.2 9.1 %collective-permute-done.9.refs_5_ = bf16[384,768]{1,0:T(8,128)(2,1)S(1)} collective-permute-done((bf16[384,768]{1,0:T(8,128)(2,1)S(1)}, bf16[384,768]{1,0:T(8,128)(2,1)S(1)}, u32[]{:S(2)}, u32[]{:S(2)}) %collective-permute-start.9) | collective-permute-done | bytes 589856 | tf_op jit(solution)/shard_map/ppermute | solution.py:76
  118.8 5.1 collective-permute-done.5.refs_1_
  127.4 4.0 collective-permute-done.7.refs_3_
  131.4 144.8 %assemble.2 = bf16[3072,768]{1,0:T(8,128)(2,1)} custom-call(s32[4]{0:T(128)} %pad_add_fusion.me_ref, bf16[384,768]{1,0:T(8,128)(2,1)} %copy-done.17, bf16[384,768]{1,0:T(8,128)(2,1)} %collective-permute-done.5.refs_1_, bf16[384,768]{1,0:T(8,128)(2,1)} %copy-done.23, bf16[384,768]{1,0:T(8,128)(2,1)} %collective-permute-done.7.refs_3_, ...), custom_call_target="tpu_custom_call" | custom-call | tf_op jit(solution)/shard_map/assemble/pallas_call | solution.py:151
  276.2 2.5 slice.172.w_out
  281.0 4.4 project.1
  285.4 25.0 %attend.1 = (bf16[1024,768]{1,0:T(8,128)(2,1)S(1)}, f32[6,8,1024]{2,1,0:T(8,128)S(1)}) custom-call(s32[1]{0:T(128)} %copy.102.count, s32[1024,1]{1,0:T(8,128)S(1)} %copy-done.6, s32[1,1024]{1,0:T(1,128)S(1)} %bitcast.170, bf16[1024,768]{1,0:T(8,128)(2,1)S(1)} %get-tuple-element.31.query, bf16[1024,768]{1,0:T(8,128)(2,1)S(1)} %get-tuple-element.32.key, ...), custom_call_target="tpu_custom_call" | custom-call | tf_op jit(solution)/shard_map/attend/pallas_call | solution.py:294
  311.6 287.7 %assemble.3 = bf16[6144,768]{1,0:T(8,128)(2,1)} custom-call(s32[4]{0:T(128)} %pad_add_fusion.me_ref, bf16[768,768]{1,0:T(8,128)(2,1)} %constant_dynamic-update-slice_fusion.10.refs_0_, bf16[768,768]{1,0:T(8,128)(2,1)} %collective-permute-done.23.refs_1_, bf16[768,768]{1,0:T(8,128)(2,1)} %collective-permute-done.24.refs_2_, ...), custom_call_target="tpu_custom_call" | custom-call | tf_op jit(solution)/shard_map/assemble/pallas_call | solution.py:151
  599.4 38.6 %middle.1 = (bf16[1024,768]{1,0:T(8,128)(2,1)}, bf16[1024,768]{1,0:T(8,128)(2,1)}, bf16[1024,3072]{1,0:T(8,128)(2,1)}, bf16[1024,3072]{1,0:T(8,128)(2,1)}, bf16[...) custom-call(s32[1]{0:T(128)} %copy.102.count, ...), custom_call_target="tpu_custom_call" | custom-call | tf_op jit(solution)/shard_map/middle/pallas_call | solution.py:480
  638.0 32.9 %attend_back.1 = (bf16[1024,768]{1,0:T(8,128)(2,1)S(1)}, bf16[1024,768]{1,0:T(8,128)(2,1)S(1)}, bf16[1024,768]{1,0:T(8,128)(2,1)S(1)}) custom-call(s32[1]{0:T(128)} %copy.102.count, s32[1024,1]{1,0:T(8,128)S(1)} %copy-done.7, s32[1,1024]{1,0:T(1,128)S(1)} %bitcast.171, bf16[1024,768]{1,0:T(8,128)(2,1)} %copy-done.3, bf16[1024,768]{1,0:T(8,128)(2,1)} %copy-done.4, ...), custom_call_target="tpu_custom_call" | custom-call | tf_op jit(solution)/shard_map/attend_back/pallas_call | solution.py:344
  694.4 8.6 %convolution_convert_fusion = bf16[3072,768]{1,0:T(8,128)(2,1)S(1)} fusion(bf16[1024,3072]{1,0:T(8,128)(2,1)} %get-tuple-element.47, bf16[1024,768]{1,0:T(8,128)(2,1)S(1)} %copy-done.30), kind=kOutput, calls=%fused_computation | convolution fusion | flops 4834197504 | bytes 12582912 | tf_op jit(solution)/shard_map/dot_general | solution.py:42
  711.1 3.6 collective-permute-start.41
  720.0 4.7 collective-permute-done.34
  726.0 7.8 collective-permute-done.32
  738.7 2.8 add_convert_fusion
  744.2 3.6 collective-permute-start.36
  749.6 14.9 %collective-permute-done.50 = bf16[2,4,96,768]{3,2,1,0:T(8,128)(2,1)S(1)} collective-permute-done((bf16[2,4,96,768]{3,2,1,0:T(8,128)(2,1)S(1)}, bf16[2,4,96,768]{3,2,1,0:T(8,128)(2,1)S(1)}, u32[]{:S(2)}, u32[]{:S(2)}) %collective-permute-start.50) | collective-permute-done | bytes 1179680 | tf_op jit(solution)/shard_map/ppermute | solution.py:76
  770.1 3.7 collective-permute-start.45
  773.9 3.5 collective-permute-done.51
  783.1 15.8 %collective-permute-done.52 = bf16[192,768]{1,0:T(8,128)(2,1)S(1)} collective-permute-done((bf16[192,768]{1,0:T(8,128)(2,1)}, bf16[192,768]{1,0:T(8,128)(2,1)S(1)}, u32[]{:S(2)}, u32[]{:S(2)}) %collective-permute-start.52) | collective-permute-done | bytes 294944 | tf_op jit(solution)/shard_map/ppermute | solution.py:76
  798.9 3.1 collective-permute-done.53
  802.0 3.2 collective-permute-done.54
  813.0 3.9 subtract_multiply_fusion
  (277 shorter events, 105.5 us)
Async XLA Ops:
  10.5 31.1 %collective-permute-start.3 = (bf16[96,768]{1,0:T(8,128)(2,1)S(1)}, bf16[96,768]{1,0:T(8,128)(2,1)S(1)}, u32[]{:S(2)}, u32[]{:S(2)}) collective-permute-start(bf16[96,768]{1,0:T(8,128)(2,1)S(1)} %convert_element_type.251), channel_id=1, source_target_pairs={{0,6},{1,7},{2,0},{3,1},{4,2},{5,3},{6,4},{7,5},{8,14},{9,15},{10,... | collective-permute-start | bytes 442376 | tf_op jit(solution)/shard_map/ppermute | solution.py:76
  11.0 30.6 %collective-permute-start.2 = (bf16[96,768]{1,0:T(8,128)(2,1)S(1)}, bf16[96,768]{1,0:T(8,128)(2,1)S(1)}, u32[]{:S(2)}, u32[]{:S(2)}) collective-permute-start(bf16[96,768]{1,0:T(8,128)(2,1)S(1)} %convert_element_type.251), channel_id=1, source_target_pairs={{0,4},{1,5},{2,6},{3,7},{4,0},{5,1},{6,2},{7,3},{8,12},{9,13},{10,... | collective-permute-start | bytes 442376 | tf_op jit(solution)/shard_map/ppermute | solution.py:76
  13.6 25.5 %collective-permute-start.1 = (bf16[96,768]{1,0:T(8,128)(2,1)S(1)}, bf16[96,768]{1,0:T(8,128)(2,1)S(1)}, u32[]{:S(2)}, u32[]{:S(2)}) collective-permute-start(bf16[96,768]{1,0:T(8,128)(2,1)S(1)} %convert_element_type.251), channel_id=1, source_target_pairs={{0,2},{1,3},{2,4},{3,5},{4,6},{5,7},{6,0},{7,1},{8,10},{9,11},{10,... | collective-permute-start | bytes 442376 | tf_op jit(solution)/shard_map/ppermute | solution.py:76
  15.8 36.5 %collective-permute-start.21 = (bf16[192,768]{1,0:T(8,128)(2,1)S(1)}, bf16[192,768]{1,0:T(8,128)(2,1)S(1)}, u32[]{:S(2)}, u32[]{:S(2)}) collective-permute-start(bf16[192,768]{1,0:T(8,128)(2,1)S(1)} %bitcast_select_fusion), channel_id=1, source_target_pairs={{0,6},{1,7},{2,0},{3,1},{4,2},{5,3},{6,4},{7,5},{8,14},{9,15},{10,... | collective-permute-start | bytes 884744 | tf_op jit(solution)/shard_map/ppermute | solution.py:76
  16.7 34.9 %collective-permute-start.20 = (bf16[192,768]{1,0:T(8,128)(2,1)S(1)}, bf16[192,768]{1,0:T(8,128)(2,1)S(1)}, u32[]{:S(2)}, u32[]{:S(2)}) collective-permute-start(bf16[192,768]{1,0:T(8,128)(2,1)S(1)} %bitcast_select_fusion), channel_id=1, source_target_pairs={{0,4},{1,5},{2,6},{3,7},{4,0},{5,1},{6,2},{7,3},{8,12},{9,13},{10,... | collective-permute-start | bytes 884744 | tf_op jit(solution)/shard_map/ppermute | solution.py:76
  54.9 16.0 %collective-permute-start.22 = (bf16[384,768]{1,0:T(8,128)(2,1)}, bf16[384,768]{1,0:T(8,128)(2,1)}, u32[]{:S(2)}, u32[]{:S(2)}) collective-permute-start(bf16[384,768]{1,0:T(8,128)(2,1)} %pad_maximum_fusion.2), channel_id=1, source_target_pairs={{0,1},{1,0},{2,3},{3,2},{4,5},{5,4},{6,7},{7,6},{8,9},{9,8},{10,11... | collective-permute-start | bytes 1769480 | tf_op jit(solution)/shard_map/ppermute | solution.py:76
  56.4 16.8 %collective-permute-start.12 = (f32[16,768]{1,0:T(8,128)S(1)}, f32[16,768]{1,0:T(8,128)S(1)}, u32[]{:S(2)}, u32[]{:S(2)}) collective-permute-start(f32[16,768]{1,0:T(8,128)S(1)} %reshape.128), channel_id=1, source_target_pairs={{0,8},{1,9},{2,10},{3,11},{4,12},{5,13},{6,14},{7,15},{8,0},{9,1},... | collective-permute-start | bytes 147464 | tf_op jit(solution)/shard_map/ppermute | solution.py:76
  56.5 51.6 %collective-permute-start.10 = (bf16[384,768]{1,0:T(8,128)(2,1)S(1)}, bf16[384,768]{1,0:T(8,128)(2,1)S(1)}, u32[]{:S(2)}, u32[]{:S(2)}) collective-permute-start(bf16[384,768]{1,0:T(8,128)(2,1)S(1)} %constant_dynamic-update-slice_fusion.5.refs_4_), channel_id=1, source_target_pairs={{0,8},{1,9},{2,10},{3,11},{4,12},{5,13},{6,14},{7,15},{8,0},{9,1},... | collective-permute-start | bytes 1769480 | tf_op jit(solution)/shard_map/ppermute | solution.py:76
  68.5 55.5 %collective-permute-start.27 = (bf16[768,768]{1,0:T(8,128)(2,1)}, bf16[768,768]{1,0:T(8,128)(2,1)}, u32[]{:S(2)}, u32[]{:S(2)}) collective-permute-start(bf16[768,768]{1,0:T(8,128)(2,1)} %constant_dynamic-update-slice_fusion.15.refs_4_), channel_id=1, source_target_pairs={{0,1},{1,0},{2,3},{3,2},{4,5},{5,4},{6,7},{7,6},{8,9},{9,8},{10,11... | collective-permute-start | bytes 3538952 | tf_op jit(solution)/shard_map/ppermute | solution.py:76
  72.9 51.6 %collective-permute-start.23 = (bf16[768,768]{1,0:T(8,128)(2,1)}, bf16[768,768]{1,0:T(8,128)(2,1)}, u32[]{:S(2)}, u32[]{:S(2)}) collective-permute-start(bf16[768,768]{1,0:T(8,128)(2,1)} %constant_dynamic-update-slice_fusion.10.refs_0_), channel_id=1, source_target_pairs={{0,16},{1,17},{2,18},{3,19},{4,20},{5,21},{6,22},{7,23},{8,24},{9,... | collective-permute-start | bytes 3538952 | tf_op jit(solution)/shard_map/ppermute | solution.py:76
  80.3 24.7 %collective-permute-start.4 = (bf16[192,768]{1,0:T(8,128)(2,1)S(1)}, bf16[192,768]{1,0:T(8,128)(2,1)S(1)}, u32[]{:S(2)}, u32[]{:S(2)}) collective-permute-start(bf16[192,768]{1,0:T(8,128)(2,1)S(1)} %pad_maximum_fusion.5), channel_id=1, source_target_pairs={{0,1},{1,0},{2,3},{3,2},{4,5},{5,4},{6,7},{7,6},{8,9},{9,8},{10,11... | collective-permute-start | bytes 884744 | tf_op jit(solution)/shard_map/ppermute | solution.py:76
  82.4 21.5 %collective-permute-start.16 = (f32[16,768]{1,0:T(8,128)S(1)}, f32[16,768]{1,0:T(8,128)S(1)}, u32[]{:S(2)}, u32[]{:S(2)}) collective-permute-start(f32[16,768]{1,0:T(8,128)S(1)} %add_add_fusion.1), channel_id=1, source_target_pairs={{0,1},{1,0},{2,3},{3,2},{4,5},{5,4},{6,7},{7,6},{8,9},{9,8},{10,11... | collective-permute-start | bytes 147464 | tf_op jit(solution)/shard_map/ppermute | solution.py:76
  118.4 193.2 %collective-permute-start.28 = (bf16[768,768]{1,0:T(8,128)(2,1)}, bf16[768,768]{1,0:T(8,128)(2,1)}, u32[]{:S(2)}, u32[]{:S(2)}) collective-permute-start(bf16[768,768]{1,0:T(8,128)(2,1)} %constant_dynamic-update-slice_fusion.15.refs_4_), channel_id=1, source_target_pairs={{0,8},{1,9},{2,10},{3,11},{4,12},{5,13},{6,14},{7,15},{8,0},{9,1},... | collective-permute-start | bytes 3538952 | tf_op jit(solution)/shard_map/ppermute | solution.py:76
  124.0 187.6 %collective-permute-start.24 = (bf16[768,768]{1,0:T(8,128)(2,1)}, bf16[768,768]{1,0:T(8,128)(2,1)}, u32[]{:S(2)}, u32[]{:S(2)}) collective-permute-start(bf16[768,768]{1,0:T(8,128)(2,1)} %constant_dynamic-update-slice_fusion.10.refs_0_), channel_id=1, source_target_pairs={{0,8},{1,9},{2,10},{3,11},{4,12},{5,13},{6,14},{7,15},{8,0},{9,1},... | collective-permute-start | bytes 3538952 | tf_op jit(solution)/shard_map/ppermute | solution.py:76
  124.0 187.6 %collective-permute-start.29 = (bf16[768,768]{1,0:T(8,128)(2,1)}, bf16[768,768]{1,0:T(8,128)(2,1)}, u32[]{:S(2)}, u32[]{:S(2)}) collective-permute-start(bf16[768,768]{1,0:T(8,128)(2,1)} %collective-permute-done.27.refs_5_), channel_id=1, source_target_pairs={{0,8},{1,9},{2,10},{3,11},{4,12},{5,13},{6,14},{7,15},{8,0},{9,1},... | collective-permute-start | bytes 3538952 | tf_op jit(solution)/shard_map/ppermute | solution.py:76
  124.5 187.1 %collective-permute-start.25 = (bf16[768,768]{1,0:T(8,128)(2,1)}, bf16[768,768]{1,0:T(8,128)(2,1)}, u32[]{:S(2)}, u32[]{:S(2)}) collective-permute-start(bf16[768,768]{1,0:T(8,128)(2,1)} %collective-permute-done.23.refs_1_), channel_id=1, source_target_pairs={{0,8},{1,9},{2,10},{3,11},{4,12},{5,13},{6,14},{7,15},{8,0},{9,1},... | collective-permute-start | bytes 3538952 | tf_op jit(solution)/shard_map/ppermute | solution.py:76
  685.0 25.7 %collective-permute-start.39 = (f32[16,768]{1,0:T(8,128)S(1)}, f32[16,768]{1,0:T(8,128)S(1)}, u32[]{:S(2)}, u32[]{:S(2)}) collective-permute-start(f32[16,768]{1,0:T(8,128)S(1)} %pad_maximum_fusion.8), channel_id=1, source_target_pairs={{0,8},{1,9},{2,10},{3,11},{4,12},{5,13},{6,14},{7,15},{8,0},{9,1},... | collective-permute-start | bytes 147464 | tf_op jit(solution)/shard_map/ppermute | solution.py:76
  692.3 16.2 %collective-permute-start.30 = (bf16[4,2,96,768]{3,2,0,1:T(8,128)(2,1)}, bf16[4,2,96,768]{3,2,0,1:T(8,128)(2,1)S(1)}, u32[]{:S(2)}, u32[]{:S(2)}) collective-permute-start(bf16[4,2,96,768]{3,2,0,1:T(8,128)(2,1)} %bitcast.162), channel_id=1, source_target_pairs={{0,8},{1,9},{2,10},{3,11},{4,12},{5,13},{6,14},{7,15},{8,0},{9,1},... | collective-permute-start | bytes 3538952 | tf_op jit(solution)/shard_map/ppermute | solution.py:76
  694.0 40.4 %collective-permute-start.46 = (bf16[4,2,192,768]{3,2,0,1:T(8,128)(2,1)}, bf16[4,2,192,768]{3,2,0,1:T(8,128)(2,1)S(1)}, u32[]{:S(2)}, u32[]{:S(2)}) collective-permute-start(bf16[4,2,192,768]{3,2,0,1:T(8,128)(2,1)} %bitcast.160), channel_id=1, source_target_pairs={{0,8},{1,9},{2,10},{3,11},{4,12},{5,13},{6,14},{7,15},{8,0},{9,1},... | collective-permute-start | bytes 7077896 | tf_op jit(solution)/shard_map/ppermute | solution.py:76
  706.4 28.7 %collective-permute-start.47 = (bf16[4,2,192,768]{3,2,0,1:T(8,128)(2,1)S(1)}, bf16[4,2,192,768]{3,2,0,1:T(8,128)(2,1)S(1)}, u32[]{:S(2)}, u32[]{:S(2)}) collective-permute-start(bf16[4,2,192,768]{3,2,0,1:T(8,128)(2,1)S(1)} %bitcast.176), channel_id=1, source_target_pairs={{0,8},{1,9},{2,10},{3,11},{4,12},{5,13},{6,14},{7,15},{8,0},{9,1},... | collective-permute-start | bytes 7077896 | tf_op jit(solution)/shard_map/ppermute | solution.py:76
  708.8 16.0 %collective-permute-start.34 = (bf16[2,4,48,768]{3,2,1,0:T(8,128)(2,1)S(1)}, bf16[2,4,48,768]{3,2,1,0:T(8,128)(2,1)S(1)}, u32[]{:S(2)}, u32[]{:S(2)}) collective-permute-start(bf16[2,4,48,768]{3,2,1,0:T(8,128)(2,1)S(1)} %fusion.56), channel_id=1, source_target_pairs={{0,1},{1,0},{2,3},{3,2},{4,5},{5,4},{6,7},{7,6},{8,9},{9,8},{10,11... | collective-permute-start | bytes 1769480 | tf_op jit(solution)/shard_map/ppermute | solution.py:76
  717.6 16.3 %collective-permute-start.32 = (bf16[4,2,48,768]{3,2,0,1:T(8,128)(2,1)S(1)}, bf16[4,2,48,768]{3,2,0,1:T(8,128)(2,1)S(1)}, u32[]{:S(2)}, u32[]{:S(2)}) collective-permute-start(bf16[4,2,48,768]{3,2,0,1:T(8,128)(2,1)S(1)} %dynamic-slice_bitcast_fusion.3), channel_id=1, source_target_pairs={{0,16},{1,17},{2,18},{3,19},{4,20},{5,21},{6,22},{7,23},{8,24},{9,... | collective-permute-start | bytes 1769480 | tf_op jit(solution)/shard_map/ppermute | solution.py:76
  719.7 21.8 %collective-permute-start.43 = (f32[16,768]{1,0:T(8,128)S(1)}, f32[16,768]{1,0:T(8,128)S(1)}, u32[]{:S(2)}, u32[]{:S(2)}) collective-permute-start(f32[16,768]{1,0:T(8,128)S(1)} %add_add_fusion), channel_id=1, source_target_pairs={{0,1},{1,0},{2,3},{3,2},{4,5},{5,4},{6,7},{7,6},{8,9},{9,8},{10,11... | collective-permute-start | bytes 147464 | tf_op jit(solution)/shard_map/ppermute | solution.py:76
  725.0 18.1 %collective-permute-start.35 = (bf16[4,48,768]{2,1,0:T(8,128)(2,1)S(1)}, bf16[4,48,768]{2,1,0:T(8,128)(2,1)S(1)}, u32[]{:S(2)}, u32[]{:S(2)}) collective-permute-start(bf16[4,48,768]{2,1,0:T(8,128)(2,1)S(1)} %dynamic-slice_bitcast_fusion.4), channel_id=1, source_target_pairs={{0,16},{1,17},{2,18},{3,19},{4,20},{5,21},{6,22},{7,23},{8,24},{9,... | collective-permute-start | bytes 884744 | tf_op jit(solution)/shard_map/ppermute | solution.py:76
  736.2 28.4 %collective-permute-start.50 = (bf16[2,4,96,768]{3,2,1,0:T(8,128)(2,1)S(1)}, bf16[2,4,96,768]{3,2,1,0:T(8,128)(2,1)S(1)}, u32[]{:S(2)}, u32[]{:S(2)}) collective-permute-start(bf16[2,4,96,768]{3,2,1,0:T(8,128)(2,1)S(1)} %fusion.30), channel_id=1, source_target_pairs={{0,1},{1,0},{2,3},{3,2},{4,5},{5,4},{6,7},{7,6},{8,9},{9,8},{10,11... | collective-permute-start | bytes 3538952 | tf_op jit(solution)/shard_map/ppermute | solution.py:76
  738.0 29.4 %collective-permute-start.48 = (bf16[4,2,96,768]{3,2,0,1:T(8,128)(2,1)S(1)}, bf16[4,2,96,768]{3,2,0,1:T(8,128)(2,1)S(1)}, u32[]{:S(2)}, u32[]{:S(2)}) collective-permute-start(bf16[4,2,96,768]{3,2,0,1:T(8,128)(2,1)S(1)} %dynamic-slice_bitcast_fusion), channel_id=1, source_target_pairs={{0,16},{1,17},{2,18},{3,19},{4,20},{5,21},{6,22},{7,23},{8,24},{9,... | collective-permute-start | bytes 3538952 | tf_op jit(solution)/shard_map/ppermute | solution.py:76
  741.5 26.4 %collective-permute-start.44 = (f32[16,768]{1,0:T(8,128)S(1)}, f32[16,768]{1,0:T(8,128)S(1)}, u32[]{:S(2)}, u32[]{:S(2)}) collective-permute-start(f32[16,768]{1,0:T(8,128)S(1)} %add.297), channel_id=1, source_target_pairs={{0,16},{1,17},{2,18},{3,19},{4,20},{5,21},{6,22},{7,23},{8,24},{9,... | collective-permute-start | bytes 147464 | tf_op jit(solution)/shard_map/ppermute | solution.py:76
  744.2 25.5 %collective-permute-start.36 = (bf16[96,768]{1,0:T(8,128)(2,1)S(1)}, bf16[96,768]{1,0:T(8,128)(2,1)S(1)}, u32[]{:S(2)}, u32[]{:S(2)}) collective-permute-start(bf16[96,768]{1,0:T(8,128)(2,1)S(1)} %get-tuple-element.76), channel_id=1, source_target_pairs={{0,2},{1,3},{2,4},{3,5},{4,6},{5,7},{6,0},{7,1},{8,10},{9,11},{10,... | collective-permute-start | bytes 442376 | tf_op jit(solution)/shard_map/ppermute | solution.py:76
  747.8 22.0 %collective-permute-start.37 = (bf16[96,768]{1,0:T(8,128)(2,1)S(1)}, bf16[96,768]{1,0:T(8,128)(2,1)S(1)}, u32[]{:S(2)}, u32[]{:S(2)}) collective-permute-start(bf16[96,768]{1,0:T(8,128)(2,1)S(1)} %get-tuple-element.77), channel_id=1, source_target_pairs={{0,4},{1,5},{2,6},{3,7},{4,0},{5,1},{6,2},{7,3},{8,12},{9,13},{10,... | collective-permute-start | bytes 442376 | tf_op jit(solution)/shard_map/ppermute | solution.py:76
  778.8 20.1 %collective-permute-start.52 = (bf16[192,768]{1,0:T(8,128)(2,1)}, bf16[192,768]{1,0:T(8,128)(2,1)S(1)}, u32[]{:S(2)}, u32[]{:S(2)}) collective-permute-start(bf16[192,768]{1,0:T(8,128)(2,1)} %get-tuple-element.73), channel_id=1, source_target_pairs={{0,2},{1,3},{2,4},{3,5},{4,6},{5,7},{6,0},{7,1},{8,10},{9,11},{10,... | collective-permute-start | bytes 884744 | tf_op jit(solution)/shard_map/ppermute | solution.py:76
  781.0 21.0 %collective-permute-start.53 = (bf16[192,768]{1,0:T(8,128)(2,1)S(1)}, bf16[192,768]{1,0:T(8,128)(2,1)S(1)}, u32[]{:S(2)}, u32[]{:S(2)}) collective-permute-start(bf16[192,768]{1,0:T(8,128)(2,1)S(1)} %get-tuple-element.74), channel_id=1, source_target_pairs={{0,4},{1,5},{2,6},{3,7},{4,0},{5,1},{6,2},{7,3},{8,12},{9,13},{10,... | collective-permute-start | bytes 884744 | tf_op jit(solution)/shard_map/ppermute | solution.py:76
  783.1 22.1 %collective-permute-start.54 = (bf16[192,768]{1,0:T(8,128)(2,1)S(1)}, bf16[192,768]{1,0:T(8,128)(2,1)}, u32[]{:S(2)}, u32[]{:S(2)}) collective-permute-start(bf16[192,768]{1,0:T(8,128)(2,1)S(1)} %get-tuple-element.75), channel_id=1, source_target_pairs={{0,6},{1,7},{2,0},{3,1},{4,2},{5,3},{6,4},{7,5},{8,14},{9,15},{10,... | collective-permute-start | bytes 884744 | tf_op jit(solution)/shard_map/ppermute | solution.py:76
  (61 other events, 779.5 us)

commit v2 on v1

v2 whole, which is shorter than its diff:
```python
import functools

import jax
import jax.numpy as jnp
from jax import lax
from jax.experimental import pallas as pl
from jax.experimental.pallas import tpu as pltpu
from jax.sharding import PartitionSpec as P

D = 768
FF = 3072
HEAD = 64
HEADS = 12
ROW = 1024
STEP = 10
CROPS = 16

NORM_EPSILON = 1e-12
NEGATIVE = -1e30
MOMENT_DECAY = 0.9
SQUARE_DECAY = 0.999
LEARN_RATE = 0.001
WEIGHT_DECAY = 0.01
ADAM_EPSILON = 1e-08
SHADOW_RATE = 0.9995
SCALE = HEAD ** (-0.5)

AXES = ("dp", "wide")
BF = jnp.bfloat16
F32 = jnp.float32
UP_CHUNKS = FF // D
ATTN_ROWS = 4 * D
FFN_ROWS = 2 * FF
ATTN_TAIL = 5 * D
FFN_TAIL = FF + 3 * D
FFN_SETS = 2
ATTEND_CALLS = 3
VEC_ROWS = 16
COUNT_ROW = 12
MIB = 1 << 20


def dot(left, right, left_dim, right_dim):
    return lax.dot_general(
        left, right, (((left_dim,), (right_dim,)), ((), ())), preferred_element_type=F32
    )


class Places:
    def __init__(self, mesh):
        self.dp, self.wide = mesh.shape["dp"], mesh.shape["wide"]
        self.count = self.dp * self.wide
        self.size = {"c": 2, "y": self.dp // 2}
        self.size["x"] = self.size["y"]
        self.size["z"] = self.wide // self.size["x"]

    def staged(self):
        exact = self.dp == 4 and self.wide % self.size["x"] == 0
        return exact and D % (16 * UP_CHUNKS * self.wide // 2) == 0

    def index(self, y, c, z, x):
        return (y * 2 + c) * self.wide + z * self.size["x"] + x

    def rotation(self, axis, step):
        pairs = []
        extent = self.size
        for y in range(extent["y"]):
            for c in range(2):
                along = axis if len(axis) == 1 else axis[c]
                for z in range(extent["z"]):
                    for x in range(extent["x"]):
                        at = {"y": y, "c": c, "z": z, "x": x}
                        to = dict(at)
                        to[along] = (at[along] + step) % extent[along]
                        pairs.append((self.index(**at), self.index(**to)))
        return pairs

    def send(self, array, axis, step):
        return lax.ppermute(array, AXES, self.rotation(axis, step))

    def here(self):
        outer, inner = lax.axis_index("dp"), lax.axis_index("wide")
        extent = self.size["x"]
        return {"y": outer // 2, "c": outer % 2, "z": inner // extent, "x": inner % extent}


def pick(array, index, axis):
    return lax.dynamic_index_in_dim(array, index, axis, keepdims=False)


def order(array, *before):
    return lax.optimization_barrier((array,) + before)[0]


class Gathered:
    def __init__(self, places, rows):
        self.places, self.rows = places, rows
        self.deep = places.size["z"] * rows

    def along_z(self, here, own):
        places, rows, extent = self.places, self.rows, self.places.size
        blocks = [own] + [places.send(own, "z", k) for k in range(1, extent["z"])]
        near = jnp.zeros((self.deep, D), BF)
        for k, block in enumerate(blocks):
            at = lax.rem(here["z"] + (extent["z"] - k), extent["z"]) * rows
            near = lax.dynamic_update_slice_in_dim(near, block[:rows], at, 0)
        if own.shape[0] > rows:
            near = jnp.concatenate([near, self.total([b[rows:] for b in blocks])], 0)
        return near

    def along_first(self, near):
        places, extent = self.places, self.places.size
        blocks = [near] + [places.send(near, "xy", k) for k in range(1, extent["x"])]
        parts = [b[: self.deep] for b in blocks]
        if near.shape[0] > self.deep:
            parts.append(self.total([b[self.deep :] for b in blocks]))
        return jnp.concatenate(parts, 0)

    def along_second(self, near):
        return [self.places.send(near, "yx", k) for k in range(1, self.places.size["x"])]

    def from_core(self, groups):
        return [self.places.send(g, "c", 1) for g in groups]

    def total(self, arrays):
        result = arrays[0].astype(F32)
        for a in arrays[1:]:
            result = result + a.astype(F32)
        return result.astype(BF)

    def columns(self, here):
        extent = self.places.size

        def back(axis, step):
            return lax.rem(here[axis] + (extent[axis] - step), extent[axis])

        for g in range(2 * extent["x"]):
            far, second = divmod(g, extent["x"])
            core = here["c"] if far == 0 else 1 - here["c"]
            for first in range(extent["x"]):
                y = jnp.where(core == 0, back("y", second), back("y", first))
                x = jnp.where(core == 0, back("x", first), back("x", second))
                yield g, first, y, core, x


def read_here(me_ref):
    return {"y": me_ref[0], "c": me_ref[1], "z": me_ref[2], "x": me_ref[3]}


class Scattered:
    def __init__(self, places, here):
        self.places, self.here, self.extent = places, here, places.size
        self.core_zero = here["c"] == 0

    def add(self, own, arrived):
        total = own.astype(F32)
        for a in arrived:
            total = total + a.astype(F32)
        return total

    def shifted(self, axis, k):
        return lax.rem(self.here[axis] + k, self.extent[axis])

    def core(self, give):
        return [self.places.send(give, "c", 1)]

    def first_cut(self, held, k):
        along_x = pick(held, self.shifted("x", k), 2).transpose(1, 0, 2, 3)
        return jnp.where(self.core_zero, along_x, pick(held, self.shifted("y", k), 0))

    def first(self, held):
        steps = range(1, self.extent["x"])
        return [self.places.send(self.first_cut(held, k), "xy", k) for k in steps]

    def second_cut(self, line, k):
        index = jnp.where(self.core_zero, self.shifted("y", k), self.shifted("x", k))
        return pick(line, index, 1)

    def second(self, line):
        steps = range(1, self.extent["x"])
        return [self.places.send(self.second_cut(line, k), "yx", k) for k in steps]

    def along_z(self, column):
        steps = range(1, self.extent["z"])
        return [self.places.send(pick(column, self.shifted("z", k), 0), "z", k) for k in steps]

    def held(self, keep, arrived):
        return self.add(keep, arrived).astype(BF)

    def line(self, held, arrived):
        return self.add(self.first_cut(held, 0), arrived).astype(BF)

    def column(self, line, arrived):
        return self.add(self.second_cut(line, 0), arrived).astype(BF)

    def result(self, column, arrived):
        return self.add(pick(column, self.here["z"], 0), arrived)


def to_rows(places, me, flat, rows, tail):
    count = places.count
    block = rows // count * D
    slack = tail // count
    before = lax.ppermute(flat[-tail:], AXES, [(i, i + 1) for i in range(count - 1)])
    joined = jnp.concatenate([before, flat])
    return lax.dynamic_slice_in_dim(joined, tail - me * slack, block).reshape(rows // count, D)


def to_flat(places, me, block, vectors, tail):
    count = places.count
    slack = tail // count
    after = lax.ppermute(block[: tail // D], AXES, [(i + 1, i) for i in range(count - 1)])
    after = jnp.where(me == count - 1, vectors, after)
    joined = jnp.concatenate([block, after], 0).reshape(-1)
    return lax.dynamic_slice_in_dim(joined, me * slack, block.size + slack)


def project_body(step, tokens, weights, vec, query, key, value):
    held = tokens[...]
    query[...] = (dot(held, weights[0:D], 1, 0) + vec[0:1]).astype(BF)
    key[...] = dot(held, weights[D : 2 * D], 1, 0).astype(BF)
    value[...] = (dot(held, weights[2 * D : 3 * D], 1, 0) + vec[1:2]).astype(BF)


def project_kernel(gathered, number, after, me, tokens, *refs):
    groups = refs[:number]
    query, key, value, vec, whole, weights, extras, sem, extra_sem, out_sem = refs[number + after :]
    step = pl.program_id(0)
    extent = gathered.places.size
    rows, deep = gathered.rows, gathered.rows * extent["z"]

    @pl.when(step == 0)
    def _():
        here = read_here(me)
        for g, ref in enumerate(groups):
            pltpu.make_async_copy(
                ref.at[pl.ds(extent["x"] * deep, VEC_ROWS)], extras.at[g], extra_sem
            ).start()
        shape = (extent["y"], 2, extent["z"], extent["x"], rows, D)
        for g, first, y, core, x in gathered.columns(here):
            pltpu.make_async_copy(
                groups[g].at[pl.ds(first * deep, deep)].reshape(extent["z"], rows, D),
                weights.reshape(*shape).at[y, core, :, x],
                sem,
            ).start()
        pltpu.make_async_copy(extras, extras, extra_sem).wait()
        total = extras[0].astype(F32)
        for g in range(1, number):
            total = total + extras[g].astype(F32)
        vec[...] = total
        pltpu.make_async_copy(weights, weights, sem).wait()
        pltpu.make_async_copy(weights, whole, out_sem).start()

    project_body(step, tokens, weights, vec, query, key, value)

    @pl.when(step == pl.num_programs(0) - 1)
    def _():
        pltpu.make_async_copy(weights, whole, out_sem).wait()


PROJECT_ROWS = 256


def project(tokens, me, gathered, groups, after):
    rows = tokens.shape[0]
    tile = pl.BlockSpec((PROJECT_ROWS, D), lambda i: (i, 0))
    number = len(groups)
    return pl.pallas_call(
        functools.partial(project_kernel, gathered, number, len(after)),
        grid=(rows // PROJECT_ROWS,),
        in_specs=[pl.BlockSpec(memory_space=pltpu.SMEM), tile]
        + [pl.BlockSpec(memory_space=pl.ANY)] * (number + len(after)),
        out_specs=[tile] * 3
        + [pl.BlockSpec((VEC_ROWS, D), lambda i: (0, 0)), pl.BlockSpec(memory_space=pl.ANY)],
        out_shape=[jax.ShapeDtypeStruct((rows, D), BF)] * 3
        + [jax.ShapeDtypeStruct((VEC_ROWS, D), F32), jax.ShapeDtypeStruct((ATTN_ROWS, D), BF)],
        scratch_shapes=[
            pltpu.VMEM((ATTN_ROWS, D), BF),
            pltpu.VMEM((number, VEC_ROWS, D), BF),
            pltpu.SemaphoreType.DMA,
            pltpu.SemaphoreType.DMA,
            pltpu.SemaphoreType.DMA,
        ],
        compiler_params=pltpu.CompilerParams(vmem_limit_bytes=24 * MIB),
        cost_estimate=cost(8),
        name="project",
    )(me, tokens, *groups, *after)


def project_whole(tokens, weights, vec):
    rows = tokens.shape[0]
    tile = pl.BlockSpec((PROJECT_ROWS, D), lambda i: (i, 0))
    return pl.pallas_call(
        lambda *refs: project_body(None, *refs),
        grid=(rows // PROJECT_ROWS,),
        in_specs=[
            tile,
            pl.BlockSpec((ATTN_ROWS, D), lambda i: (0, 0), pipeline_mode=pl.Buffered(1)),
            pl.BlockSpec((VEC_ROWS, D), lambda i: (0, 0)),
        ],
        out_specs=[tile] * 3,
        out_shape=[jax.ShapeDtypeStruct((rows, D), BF)] * 3,
        compiler_params=pltpu.CompilerParams(vmem_limit_bytes=24 * MIB),
        name="project",
    )(tokens, weights, vec)


QUERY_BLOCK = 256
QUERY_BLOCKS = ROW // QUERY_BLOCK


def window(block):
    low = max(0, block - 1) * QUERY_BLOCK
    return low, min(QUERY_BLOCKS, block + 2) * QUERY_BLOCK


def fill_bias(bias, seg_column, seg_row, count):
    for block in range(QUERY_BLOCKS):
        low, high = window(block)
        at = slice(block * QUERY_BLOCK, (block + 1) * QUERY_BLOCK)
        shape = (high - low, QUERY_BLOCK)
        key_pos = low + lax.broadcasted_iota(jnp.int32, shape, 0)
        query_pos = block * QUERY_BLOCK + lax.broadcasted_iota(jnp.int32, shape, 1)
        same = seg_column[low:high, 0:1] == seg_row[0:1, at]
        allowed = (same & (key_pos < count)) | (key_pos == query_pos)
        bias[0 : high - low, at] = jnp.where(allowed, 0.0, NEGATIVE).astype(F32)


def one_head(transposed):
    zero = jnp.zeros((HEAD, transposed.shape[1]), transposed.dtype)
    return (
        jnp.concatenate([transposed[:HEAD], zero], 0),
        jnp.concatenate([zero, transposed[HEAD:]], 0),
    )


def attend_kernel(count, seg_column, seg_row, query, key, value, *refs):
    mixed, log_total, bias = refs[-3:]

    @pl.when(pl.program_id(0) == 0)
    def _():
        fill_bias(bias, seg_column, seg_row, count[0])

    value_t = value[...].T
    query_t = one_head((query[...] * jnp.asarray(SCALE, BF)).T)
    for block in range(QUERY_BLOCKS):
        low, high = window(block)
        at = slice(block * QUERY_BLOCK, (block + 1) * QUERY_BLOCK)
        parts = []
        for h in range(2):
            scores = dot(key[low:high, :], query_t[h][:, at], 1, 0) + bias[0 : high - low, at]
            top = jnp.max(scores, axis=0, keepdims=True)
            shifted = jnp.exp(scores - top)
            total = jnp.sum(shifted, axis=0, keepdims=True)
            part = dot(value_t[h * HEAD : (h + 1) * HEAD, low:high], shifted.astype(BF), 1, 0)
            parts.append(part * (1.0 / total))
            log_total[0, h : h + 1, at] = top + jnp.log(total)
        mixed[at, :] = jnp.concatenate(parts, 0).T.astype(BF)


def attend_specs():
    return [
        pl.BlockSpec(memory_space=pltpu.SMEM),
        pl.BlockSpec((ROW, 1), lambda h: (0, 0)),
        pl.BlockSpec((1, ROW), lambda h: (0, 0)),
    ]


def attend(query, key, value, segments, count, first, pairs, after):
    pair = pl.BlockSpec((ROW, 2 * HEAD), lambda h: (0, h + first))
    return pl.pallas_call(
        attend_kernel,
        grid=(pairs,),
        in_specs=attend_specs() + [pair] * 3 + [pl.BlockSpec(memory_space=pl.ANY)] * len(after),
        out_specs=[
            pl.BlockSpec((ROW, 2 * HEAD), lambda h: (0, h)),
            pl.BlockSpec((1, 8, ROW), lambda h: (h, 0, 0)),
        ],
        out_shape=[
            jax.ShapeDtypeStruct((ROW, pairs * 2 * HEAD), BF),
            jax.ShapeDtypeStruct((pairs, 8, ROW), F32),
        ],
        scratch_shapes=[pltpu.VMEM((3 * QUERY_BLOCK, ROW), F32)],
        compiler_params=pltpu.CompilerParams(vmem_limit_bytes=24 * MIB),
        cost_estimate=cost(25 * pairs / 6),
        name="attend",
    )(count, segments.reshape(ROW, 1), segments.reshape(1, ROW), query, key, value, *after)


def attend_back_kernel(
    count, seg_column, seg_row, query, key, value, grad, log_total, *refs
):
    grads, sums, bias, key_sum, value_sum = refs[-5:]

    @pl.when(pl.program_id(0) == 0)
    def _():
        fill_bias(bias, seg_column, seg_row, count[0])

    query_t = (query[...] * jnp.asarray(SCALE, BF)).T
    key_t = key[...].T
    grad_t = grad[...].T
    query_one, grad_one = one_head(query_t), one_head(grad_t)
    key_sum[...] = jnp.zeros_like(key_sum)
    value_sum[...] = jnp.zeros_like(value_sum)
    for block in range(QUERY_BLOCKS):
        low, high = window(block)
        at = slice(block * QUERY_BLOCK, (block + 1) * QUERY_BLOCK)
        parts = []
        for h in range(2):
            rows = slice(h * HEAD, (h + 1) * HEAD)
            scores = dot(key[low:high, :], query_one[h][:, at], 1, 0) + bias[0 : high - low, at]
            probs = jnp.exp(scores - log_total[0, h : h + 1, at])
            grad_probs = dot(value[low:high, :], grad_one[h][:, at], 1, 0)
            weighted = probs * grad_probs
            total = jnp.sum(weighted, axis=0, keepdims=True)
            grad_scores = (weighted - probs * total).astype(BF)
            parts.append(dot(key_t[rows, low:high], grad_scores, 1, 0))
            key_sum[rows, low:high] += dot(query_t[rows, at], grad_scores, 1, 1)
            value_sum[rows, low:high] += dot(grad_t[rows, at], probs.astype(BF), 1, 1)
        grads[0, at, :] = (jnp.concatenate(parts, 0) * SCALE).T.astype(BF)
    grads[1] = key_sum[...].T.astype(BF)
    grads[2] = value_sum[...].T.astype(BF)
    sums[...] = jnp.zeros_like(sums)
    sums[0:1] = column_sum(grads[0].astype(F32))
    sums[1:2] = column_sum(grads[2].astype(F32))


def attend_back(query, key, value, grad, log_total, segments, count, first, pairs, after):
    pair = pl.BlockSpec((ROW, 2 * HEAD), lambda h: (0, h + first))
    return pl.pallas_call(
        attend_back_kernel,
        grid=(pairs,),
        in_specs=attend_specs()
        + [pair] * 4
        + [pl.BlockSpec((1, 8, ROW), lambda h: (h, 0, 0))]
        + [pl.BlockSpec(memory_space=pl.ANY)] * len(after),
        out_specs=[
            pl.BlockSpec((3, ROW, 2 * HEAD), lambda h: (0, 0, h)),
            pl.BlockSpec((8, 2 * HEAD), lambda h: (0, h)),
        ],
        out_shape=[
            jax.ShapeDtypeStruct((3, ROW, pairs * 2 * HEAD), BF),
            jax.ShapeDtypeStruct((8, pairs * 2 * HEAD), F32),
        ],
        scratch_shapes=[
            pltpu.VMEM((3 * QUERY_BLOCK, ROW), F32),
            pltpu.VMEM((2 * HEAD, ROW), F32),
            pltpu.VMEM((2 * HEAD, ROW), F32),
        ],
        compiler_params=pltpu.CompilerParams(vmem_limit_bytes=24 * MIB),
        cost_estimate=cost(33 * pairs / 6),
        name="attend_back",
    )(
        count,
        segments.reshape(ROW, 1),
        segments.reshape(1, ROW),
        query,
        key,
        value,
        grad,
        log_total,
        *after,
    )


def normalise(resid):
    centred = resid - jnp.mean(resid, axis=-1, keepdims=True)
    spread = jnp.mean(centred * centred, axis=-1, keepdims=True)
    inverse = lax.rsqrt(spread + NORM_EPSILON)
    return centred * inverse, inverse


def normalise_back(cotangent, gain, normal, inverse):
    scaled = cotangent * gain
    mean = jnp.mean(scaled, axis=-1, keepdims=True)
    aligned = jnp.mean(scaled * normal, axis=-1, keepdims=True)
    return inverse * (scaled - mean - normal * aligned)


def cost(micros):
    return pl.CostEstimate(flops=int(micros * 1.1e9), bytes_accessed=MIB, transcendentals=0)


def column_sum(array):
    return jnp.sum(array, axis=0, keepdims=True)


MIDDLE_ROWS = 256


def middle_kernel(
    fetch,
    groups,
    count,
    me,
    seg_row,
    tokens,
    out_grad,
    w_out,
    vec,
    *refs,
):
    mixed = jnp.concatenate([ref[...] for ref in refs[:ATTEND_CALLS]], 1)
    refs = refs[ATTEND_CALLS:]
    (
        final_low,
        hidden_low,
        activated,
        grad_pre,
        grad_ffn_out,
        grad_attn_out,
        grad_mixed,
        grad_resid,
        vec_grad,
        crop_sums,
        slope,
        weights,
        sem,
    ) = refs[groups:]
    step = pl.program_id(0)

    @pl.when(step == 0)
    def _():
        vec_grad[...] = jnp.zeros_like(vec_grad)
        crop_sums[...] = jnp.zeros_like(crop_sums)
        fetch(read_here(me), refs[:groups], weights, sem)

    def row(i):
        return vec[i : i + 1]

    def chunk(j):
        return weights[j * D : (j + 1) * D]

    def note(i, value):
        vec_grad[i : i + 1] += value

    resid_one = tokens[...].astype(F32) + (dot(mixed, w_out[...], 1, 0) + row(2))
    normal_one, inverse_one = normalise(resid_one)
    hidden = normal_one * row(3) + row(4)
    low = hidden.astype(BF)
    hidden_low[...] = low
    total = hidden + row(9)

    def arrived(first, chunks, which):
        @pl.when(step == 0)
        def _():
            part = weights.at[pl.ds(first * D, chunks * D)]
            pltpu.make_async_copy(part, part, sem.at[which]).wait()

    for j in range(UP_CHUNKS):
        at = slice(j * D, (j + 1) * D)
        arrived(j, 1, j)
        pre = dot(low, chunk(j), 1, 0) + row(5 + j)
        share = 0.5 + 0.5 * lax.erf(pre * (0.5**0.5))
        density = jnp.exp(-0.5 * pre * pre) * 0.3989422804014327
        slope[:, at] = share + pre * density
        act = (pre * share).astype(BF)
        activated[:, at] = act
        if j == 0:
            arrived(UP_CHUNKS, UP_CHUNKS, UP_CHUNKS)
        total = total + dot(act, chunk(UP_CHUNKS + j), 1, 0)
    normal_two, inverse_two = normalise(total)
    final = normal_two * row(10) + row(11)
    final_low[...] = final.astype(BF)

    first = step * MIDDLE_ROWS
    across = (CROPS, MIDDLE_ROWS)
    position = first + lax.broadcasted_iota(jnp.int32, across, 1)
    crop = lax.broadcasted_iota(jnp.int32, across, 0)
    member = ((seg_row[...] == crop) & (position < count[0])).astype(BF)
    high = final.astype(BF)
    rest = final - high.astype(F32)
    mid = rest.astype(BF)
    tiny = (rest - mid.astype(F32)).astype(BF)
    crop_sums[...] += dot(member, high, 1, 0) + (dot(member, mid, 1, 0) + dot(member, tiny, 1, 0))

    position = first + lax.broadcasted_iota(jnp.int32, (MIDDLE_ROWS, 1), 0)
    valid = (position < count[0]).astype(F32)
    cotangent = out_grad[...].astype(F32) * valid
    note(10, column_sum(cotangent * normal_two))
    note(11, column_sum(cotangent))
    grad_two = normalise_back(cotangent, row(10), normal_two, inverse_two)
    grad_out = grad_two.astype(BF)
    grad_ffn_out[...] = grad_out
    note(9, column_sum(grad_out.astype(F32)))
    grad_hidden = grad_two
    for j in range(UP_CHUNKS):
        at = slice(j * D, (j + 1) * D)
        back = (dot(grad_out, chunk(UP_CHUNKS + j), 1, 1) * slope[:, at]).astype(BF)
        grad_pre[:, at] = back
        note(5 + j, column_sum(back.astype(F32)))
        grad_hidden = grad_hidden + dot(back, chunk(j), 1, 1)
    note(3, column_sum(grad_hidden * normal_one))
    note(4, column_sum(grad_hidden))
    grad_one = normalise_back(grad_hidden, row(3), normal_one, inverse_one)
    grad_resid[...] = grad_one
    grad_proj = grad_one.astype(BF)
    grad_attn_out[...] = grad_proj
    note(2, column_sum(grad_proj.astype(F32)))
    grad_mixed[...] = dot(grad_proj, w_out[...], 1, 1).astype(BF)


def middle(count, me, segments, mixed, tokens, out_grad, attn_whole, sources, fetch, vec):
    rows = tokens.shape[0]
    tile = pl.BlockSpec((MIDDLE_ROWS, D), lambda i: (i, 0))
    wide = pl.BlockSpec((MIDDLE_ROWS, FF), lambda i: (i, 0))
    small = pl.BlockSpec((VEC_ROWS, D), lambda i: (0, 0))

    def shape(width, kind):
        return jax.ShapeDtypeStruct((rows, width), kind)

    return pl.pallas_call(
        functools.partial(middle_kernel, fetch, len(sources)),
        grid=(rows // MIDDLE_ROWS,),
        in_specs=[
            pl.BlockSpec(memory_space=pltpu.SMEM),
            pl.BlockSpec(memory_space=pltpu.SMEM),
            pl.BlockSpec((1, MIDDLE_ROWS), lambda i: (0, i)),
            tile,
            tile,
            pl.BlockSpec((D, D), lambda i: (3, 0), pipeline_mode=pl.Buffered(1)),
            small,
        ]
        + [pl.BlockSpec((MIDDLE_ROWS, D // ATTEND_CALLS), lambda i: (i, 0))] * ATTEND_CALLS
        + [pl.BlockSpec(memory_space=pl.ANY)] * len(sources),
        out_specs=[tile, tile, wide, wide, tile, tile, tile, tile, small, small],
        out_shape=[
            shape(D, BF),
            shape(D, BF),
            shape(FF, BF),
            shape(FF, BF),
            shape(D, BF),
            shape(D, BF),
            shape(D, BF),
            shape(D, F32),
            jax.ShapeDtypeStruct((VEC_ROWS, D), F32),
            jax.ShapeDtypeStruct((CROPS, D), F32),
        ],
        scratch_shapes=[
            pltpu.VMEM((MIDDLE_ROWS, FF), F32),
            pltpu.VMEM((FFN_ROWS, D), BF),
            pltpu.SemaphoreType.DMA((UP_CHUNKS + 1,)),
        ],
        compiler_params=pltpu.CompilerParams(vmem_limit_bytes=44 * MIB),
        cost_estimate=cost(40),
        name="middle",
    )(count, me, segments.reshape(1, rows), tokens, out_grad, attn_whole, vec, *mixed, *sources)


WIDTH = 2 * HEAD * (HEADS // 2 // 3)


def ffn_terms_kernel(shares, me, hidden, activated, *refs):
    pre, out = refs[:shares], refs[shares : 2 * shares]
    keep, give, hidden_t, block, sem = refs[-5:]
    step = pl.program_id(0)
    slot = lax.rem(step, 2)
    owners, rows = keep.shape[1], keep.shape[2]
    up_rows = rows // UP_CHUNKS
    per_chunk = D // rows

    @pl.when(step == 0)
    def _():
        hidden_t[...] = hidden[...].T

    @pl.when(step >= 2)
    def _():
        pltpu.make_async_copy(block.at[slot], block.at[slot], sem.at[slot]).wait()

    def to(core, y, start):
        @pl.when(core == me[1])
        def _():
            start(keep.at[y])

        @pl.when(core != me[1])
        def _():
            start(give.at[y])

    @pl.when(step < UP_CHUNKS)
    def _():
        right = jnp.concatenate([ref[...] for ref in pre], 1)
        block[slot] = dot(hidden_t[...], right, 1, 0).astype(BF)
        for core in range(2):
            source = block.at[slot, pl.ds(core * (D // 2), D // 2)]
            source = source.reshape(owners, up_rows, block.shape[2])

            def start(target):
                at = pl.ds(pl.multiple_of(step * up_rows, 16), up_rows)
                pltpu.make_async_copy(source, target.at[:, at], sem.at[slot]).start()

            to(core, 0, start)

    @pl.when(step >= UP_CHUNKS)
    def _():
        right = jnp.concatenate([ref[...] for ref in out], 1)
        block[slot] = dot(activated[...], right, 0, 0).astype(BF)
        chunk = step - UP_CHUNKS
        source = block.at[slot].reshape(per_chunk, rows, block.shape[2])

        def start(target):
            at = pl.ds(lax.rem(chunk, 2) * per_chunk, per_chunk)
            pltpu.make_async_copy(source, target.at[at], sem.at[slot]).start()

        to(lax.div(chunk, 2), 1, start)

    @pl.when(step == pl.num_programs(0) - 1)
    def _():
        for s in range(2):
            pltpu.make_async_copy(block.at[s], block.at[s], sem.at[s]).wait()


def ffn_terms(places, me, hidden, activated, grad_pre, grad_out, thirds, after):
    owners = places.wide
    rows = FFN_ROWS // places.count
    shares = len(thirds)
    width = shares * WIDTH
    shape = jax.ShapeDtypeStruct((2, owners, rows, width), BF)

    def pre_spec(third):
        return pl.BlockSpec((ROW, WIDTH), lambda i: (0, 3 * jnp.minimum(i, UP_CHUNKS - 1) + third))

    def out_spec(third):
        return pl.BlockSpec((ROW, WIDTH), lambda i: (0, third))

    def kernel(me_ref, hidden_ref, activated_ref, *refs):
        used = refs[: 2 * shares] + refs[2 * shares + len(after) :]
        ffn_terms_kernel(shares, me_ref, hidden_ref, activated_ref, *used)

    return pl.pallas_call(
        kernel,
        grid=(2 * UP_CHUNKS,),
        in_specs=[
            pl.BlockSpec(memory_space=pltpu.SMEM),
            pl.BlockSpec((ROW, D), lambda i: (0, 0), pipeline_mode=pl.Buffered(1)),
            pl.BlockSpec((ROW, D), lambda i: (0, jnp.maximum(i - UP_CHUNKS, 0))),
        ]
        + [pre_spec(t) for t in thirds]
        + [out_spec(t) for t in thirds]
        + [pl.BlockSpec(memory_space=pl.ANY)] * len(after),
        out_specs=[pl.BlockSpec(memory_space=pl.ANY)] * 2,
        out_shape=[shape] * 2,
        scratch_shapes=[
            pltpu.VMEM((D, ROW), BF),
            pltpu.VMEM((2, D, width), BF),
            pltpu.SemaphoreType.DMA((2,)),
        ],
        compiler_params=pltpu.CompilerParams(vmem_limit_bytes=32 * MIB),
        cost_estimate=cost(5 * shares),
        name="ffn_terms",
    )(me, hidden, activated, *([grad_pre] * shares), *([grad_out] * shares), *after)


def attn_terms(places, me, tokens, mixed, grads, grad_proj, thirds, vectors, after):
    owners = places.wide
    rows = ATTN_ROWS // places.count
    shares, extra = len(thirds), vectors.shape[0]
    width = shares * WIDTH
    shape = jax.ShapeDtypeStruct((2, owners, rows + extra, width), BF)

    def kernel(me_ref, tokens_ref, vectors_ref, *refs):
        mixed_refs, refs = refs[:ATTEND_CALLS], refs[ATTEND_CALLS:]
        grad_refs, proj_refs, refs = refs[:shares], refs[shares : 2 * shares], refs[2 * shares :]
        keep, give, tokens_t, block, below, sem, below_sem = refs[len(after) :]
        step = pl.program_id(0)
        slot = lax.rem(step, 2)

        @pl.when(step == 0)
        def _():
            tokens_t[...] = tokens_ref[...].T
            below[...] = jnp.broadcast_to(vectors_ref[...][None], below.shape)
            for target in (keep, give):
                for y in range(2):
                    pltpu.make_async_copy(
                        below, target.at[y, :, pl.ds(rows, extra)], below_sem
                    ).start()

        @pl.when(step >= 2)
        def _():
            pltpu.make_async_copy(block.at[slot], block.at[slot], sem.at[slot]).wait()

        @pl.when(step < 3)
        def _():
            right = jnp.concatenate([ref[0] for ref in grad_refs], 1)
            block[slot] = dot(tokens_t[...], right, 1, 0).astype(BF)

        @pl.when(step == 3)
        def _():
            left = jnp.concatenate([ref[...] for ref in mixed_refs], 1)
            right = jnp.concatenate([ref[...] for ref in proj_refs], 1)
            block[slot] = dot(left, right, 0, 0).astype(BF)

        source = block.at[slot].reshape(owners, rows, width)
        y, core = lax.div(step, 2), lax.rem(step, 2)

        @pl.when(core == me_ref[1])
        def _():
            pltpu.make_async_copy(source, keep.at[y, :, pl.ds(0, rows)], sem.at[slot]).start()

        @pl.when(core != me_ref[1])
        def _():
            pltpu.make_async_copy(source, give.at[y, :, pl.ds(0, rows)], sem.at[slot]).start()

        @pl.when(step == 3)
        def _():
            for s in range(2):
                pltpu.make_async_copy(block.at[s], block.at[s], sem.at[s]).wait()
            for _ in range(4):
                pltpu.make_async_copy(below, below, below_sem).wait()

    def third_spec(third):
        return pl.BlockSpec((ROW, WIDTH), lambda i: (0, third))

    return pl.pallas_call(
        kernel,
        grid=(4,),
        in_specs=[
            pl.BlockSpec(memory_space=pltpu.SMEM),
            pl.BlockSpec((ROW, D), lambda i: (0, 0), pipeline_mode=pl.Buffered(1)),
            pl.BlockSpec((extra, width), lambda i: (0, 0)),
        ]
        + [pl.BlockSpec((ROW, WIDTH), lambda i: (0, 0), pipeline_mode=pl.Buffered(1))] * ATTEND_CALLS
        + [pl.BlockSpec((1, ROW, WIDTH), lambda i: (jnp.minimum(i, 2), 0, 0))] * shares
        + [third_spec(t) for t in thirds]
        + [pl.BlockSpec(memory_space=pl.ANY)] * len(after),
        out_specs=[pl.BlockSpec(memory_space=pl.ANY)] * 2,
        out_shape=[shape] * 2,
        scratch_shapes=[
            pltpu.VMEM((D, ROW), BF),
            pltpu.VMEM((2, D, width), BF),
            pltpu.VMEM((owners, extra, width), BF),
            pltpu.SemaphoreType.DMA((2,)),
            pltpu.SemaphoreType.DMA,
        ],
        compiler_params=pltpu.CompilerParams(vmem_limit_bytes=24 * MIB),
        cost_estimate=cost(1.5 * shares + 1),
        name="attn_terms",
    )(me, tokens, vectors, *mixed, *grads, *([grad_proj] * shares), *after)


def token_grad_kernel(resid, weights, *refs):
    out = refs[-1]
    total = resid[...]
    for i, ref in enumerate(refs[:ATTEND_CALLS]):
        for m in range(3):
            held = weights[m * D : (m + 1) * D, i * WIDTH : (i + 1) * WIDTH]
            total = total + dot(ref[m], held, 1, 1)
    out[...] = total.astype(BF)


def token_gradient(resid, weights, grads, after):
    step = 256
    tile = pl.BlockSpec((step, D), lambda i: (i, 0))
    return pl.pallas_call(
        token_grad_kernel,
        grid=(ROW // step,),
        in_specs=[tile, pl.BlockSpec((3 * D, D), lambda i: (0, 0), pipeline_mode=pl.Buffered(1))]
        + [pl.BlockSpec((3, step, WIDTH), lambda i: (0, i, 0))] * ATTEND_CALLS
        + [pl.BlockSpec(memory_space=pl.ANY)] * len(after),
        out_specs=tile,
        out_shape=jax.ShapeDtypeStruct((ROW, D), BF),
        compiler_params=pltpu.CompilerParams(vmem_limit_bytes=24 * MIB),
        cost_estimate=cost(5),
        name="token_grad",
    )(resid, weights, *grads, *after)


def adam_update(param, gradient, moment, square, shadow):
    step_float = float(STEP)
    moment_next = MOMENT_DECAY * moment + (1.0 - MOMENT_DECAY) * gradient
    square_next = SQUARE_DECAY * square + (1.0 - SQUARE_DECAY) * gradient * gradient
    moment_hat = moment_next / (1.0 - MOMENT_DECAY**step_float)
    square_hat = square_next / (1.0 - SQUARE_DECAY**step_float)
    change = -LEARN_RATE * (
        moment_hat / (jnp.sqrt(square_hat) + ADAM_EPSILON) + WEIGHT_DECAY * param
    )
    updated = param + change
    drift = (1.0 - SHADOW_RATE) * (updated - shadow)
    return (change, moment_next, square_next, drift)


def contract_rows(left, right):
    return dot(left, right, 0, 0)


def on_device(
    places,
    tokens,
    segments,
    counts,
    out_grad,
    attn_param,
    attn_moment,
    attn_square,
    attn_shadow,
    ffn_param,
    ffn_moment,
    ffn_square,
    ffn_shadow,
):
    assert counts.shape[0] == 1 and tokens.shape[0] == ROW
    number = places.count
    here = places.here()
    place_list = jnp.stack([here[a] for a in ("y", "c", "z", "x")]).astype(jnp.int32)
    me = lax.axis_index("dp") * places.wide + lax.axis_index("wide")
    staged = places.staged()
    attn_rows, ffn_rows = ATTN_ROWS // number, FFN_ROWS // number
    up_rows = ffn_rows // UP_CHUNKS
    holds_up = me < number // 2

    last = me == number - 1
    ends = jnp.concatenate([attn_param[-ATTN_TAIL:], ffn_param[-FFN_TAIL:]]).astype(BF)
    ends = jnp.where(last, ends, jnp.zeros_like(ends))
    if staged:
        digits = [lax.rem(lax.shift_right_logical(counts[0], 3 * i), 8) for i in range(4)]
        count_row = jnp.concatenate([jnp.stack(digits).astype(BF), jnp.zeros((D - 4,), BF)])
        filler = jnp.zeros(((VEC_ROWS - COUNT_ROW - 1) * D,), BF)
        extra = jnp.concatenate([ends, count_row, filler]).reshape(VEC_ROWS, D)
        attn_own = to_rows(places, me, attn_param, ATTN_ROWS, ATTN_TAIL).astype(BF)
        attn_set = Gathered(places, attn_rows)
        column = attn_set.along_z(here, jnp.concatenate([attn_own, extra], 0))
        ffn_own = to_rows(places, me, order(ffn_param, column), FFN_ROWS, FFN_TAIL).astype(BF)
        by_chunk = ffn_own.reshape(up_rows, UP_CHUNKS, D).transpose(1, 0, 2).reshape(ffn_rows, D)
        ffn_own = jnp.where(holds_up, by_chunk, ffn_own)
        plane = attn_set.along_first(column)
        groups = [plane] + attn_set.along_second(plane)
        attn_groups = groups + attn_set.from_core(groups)
        set_rows = ffn_rows // FFN_SETS
        per_set = UP_CHUNKS // FFN_SETS
        ffn_set = Gathered(places, set_rows)
        columns = [
            ffn_set.along_z(here, ffn_own[i * set_rows : (i + 1) * set_rows])
            for i in range(FFN_SETS)
        ]
        query, key, value, vec, attn_whole = project(
            tokens, place_list, attn_set, attn_groups, columns
        )
        token_total = sum(vec[COUNT_ROW, i] * float(8**i) for i in range(4))
        planes = [order(ffn_set.along_first(c), query) for c in columns]
        groups = [[p] + [order(g, query) for g in ffn_set.from_core([p])] for p in planes]
        far = [ffn_set.along_second(p) for p in planes]
        attend_after = [[planes[0]], [planes[1]], []]
        extent = places.size
        piece = (extent["x"], extent["z"], per_set, up_rows, D)
        half = extent["y"] // 2

        def fetch(place, refs, weights, sem):
            side = (half, 2, extent["z"], extent["x"])
            up = weights.at[pl.ds(0, FF)].reshape(*((UP_CHUNKS,) + side + (up_rows, D)))
            down = weights.at[pl.ds(FF, FF)].reshape(*(side + (UP_CHUNKS, up_rows, D)))
            number = 2 * extent["x"]
            for s in range(FFN_SETS):
                own = refs[s * number : (s + 1) * number]
                chunks = pl.ds(s * per_set, per_set)
                for g, first, y, core, x in ffn_set.columns(place):

                    @pl.when(y < half)
                    def _():
                        for part in range(per_set):
                            chunk = s * per_set + part
                            pltpu.make_async_copy(
                                own[g].at[first, :, part],
                                up.at[chunk, y, core, :, x],
                                sem.at[chunk],
                            ).start()

                    @pl.when(y >= half)
                    def _():
                        pltpu.make_async_copy(
                            own[g].at[first],
                            down.at[y - half, core, :, x, chunks],
                            sem.at[UP_CHUNKS],
                        ).start()

    else:
        token_total = lax.psum(counts[0].astype(F32), AXES)
        vec = lax.psum(ends.astype(F32), AXES).reshape(COUNT_ROW, D)
        vec = jnp.concatenate([vec, jnp.zeros((VEC_ROWS - COUNT_ROW, D), F32)], 0)
        flat = lax.all_gather(attn_param.astype(BF), AXES, axis=0, tiled=True)
        attn_whole = flat[: ATTN_ROWS * D].reshape(ATTN_ROWS, D)
        flat = lax.all_gather(ffn_param.astype(BF), AXES, axis=0, tiled=True)
        w_up = flat[: FF * D].reshape(D, UP_CHUNKS, D).transpose(1, 0, 2).reshape(FF, D)
        w_down = flat[FF * D : FFN_ROWS * D].reshape(FF, D)
        sources = [w_up, w_down]

        def fetch(place, refs, weights, sem):
            w_up, w_down = refs
            for j in range(UP_CHUNKS):
                rows = pl.ds(j * D, D)
                pltpu.make_async_copy(w_up.at[rows], weights.at[rows], sem.at[j]).start()
            down = weights.at[pl.ds(FF, FF)]
            pltpu.make_async_copy(w_down, down, sem.at[UP_CHUNKS]).start()

        query, key, value = project_whole(tokens, attn_whole, vec)
        attend_after = [[]] * ATTEND_CALLS

    pairs = HEADS // 2 // ATTEND_CALLS
    ahead = [
        attend(query, key, value, segments, counts, i * pairs, pairs, attend_after[i])
        for i in range(ATTEND_CALLS)
    ]
    mixed = [a[0] for a in ahead]
    if staged:
        sources = []
        for s in range(FFN_SETS):
            near, crossed = groups[s]
            others = [order(f, mixed[s + 1]) for f in far[s]]
            arrays = [near] + others + [crossed] + ffn_set.from_core(others)
            sources += [g.reshape(piece) for g in arrays]
    (
        final_low,
        hidden_low,
        activated,
        grad_pre,
        grad_ffn_out,
        grad_attn_out,
        grad_mixed,
        grad_resid,
        vec_grad,
        crop_sums,
    ) = middle(
        counts,
        place_list,
        segments,
        mixed,
        tokens,
        out_grad,
        attn_whole,
        sources,
        fetch,
        vec,
    )
    is_valid = jnp.arange(ROW, dtype=jnp.int32) < counts[0]
    member = (segments[None, :] == jnp.arange(CROPS, dtype=jnp.int32)[:, None]) & is_valid[None, :]
    crop_sizes = jnp.sum(member.astype(F32), axis=1)
    pooled = crop_sums / jnp.maximum(crop_sizes, 1.0)[:, None]

    def back(i, after):
        return attend_back(
            query,
            key,
            value,
            grad_mixed,
            ahead[i][1],
            segments,
            counts,
            i * pairs,
            pairs,
            after,
        )

    if staged:
        sums = Scattered(places, here)

        def spread(terms):
            return terms.reshape(2, extent["z"], extent["x"], *terms.shape[2:])

        def ffn_side(thirds, after):
            operands = (hidden_low, activated, grad_pre, grad_ffn_out)
            terms = ffn_terms(places, place_list, *operands, thirds, after)
            return [spread(t) for t in terms]

        def attn_side(thirds, grads, vectors, after):
            width = len(thirds) * WIDTH
            vectors = vectors.astype(BF).reshape(-1)
            filled = -(-vectors.shape[0] // (16 * width)) * 16
            vectors = jnp.pad(vectors, (0, filled * width - vectors.shape[0]))
            vectors = vectors.reshape(filled, width)
            operands = (tokens, mixed, grads, grad_attn_out)
            terms = attn_terms(places, place_list, *operands, thirds, vectors, after)
            return [spread(t) for t in terms]

        def later(arrays, *before):
            return [order(a, *before) for a in arrays]

        keep_a, give_a = ffn_side([0, 1], [])
        core_a = sums.core(give_a)
        keep_b, give_b = ffn_side([2], [give_a])
        core_b = sums.core(give_b)
        held_a = sums.held(keep_a, later(core_a, give_b))
        first_a = sums.first(held_a)
        held_b = sums.held(keep_b, later(core_b, held_a))
        first_b = sums.first(held_b)
        back_0 = back(0, [held_a, held_b])
        line_a = sums.line(held_a, later(first_a, back_0[0]))
        line_b = sums.line(held_b, later(first_b, back_0[0]))
        second_a, second_b = sums.second(line_a), sums.second(line_b)
        back_1 = back(1, [line_a, line_b])
        column_a = sums.column(line_a, later(second_a, back_1[0]))
        column_b = sums.column(line_b, later(second_b, back_1[0]))
        up_z_a, up_z_b = sums.along_z(column_a), sums.along_z(column_b)
        grads = [back_0[0], back_1[0]]
        keep_c, give_c = attn_side([0, 1], grads, vec_grad[2:12], [column_a, column_b])
        core_c = sums.core(give_c)
        back_2 = back(2, [give_c])
        held_c = sums.held(keep_c, later(core_c, back_2[0]))
        first_c = sums.first(held_c)
        vectors = jnp.stack(
            [jnp.concatenate([b[1][i] for b in (back_0, back_1, back_2)]) for i in range(2)]
        )
        grads = [b[0] for b in (back_0, back_1, back_2)]
        keep_d, give_d = attn_side([2], grads[2:], vectors, [held_c])
        core_d = sums.core(give_d)
        token_grad = token_gradient(grad_resid, attn_whole, grads, [give_d])
        held_d = sums.held(keep_d, core_d)
        first_d = sums.first(held_d)
        line_c = sums.line(held_c, later(first_c, give_d))
        second_c = sums.second(line_c)
        line_d = sums.line(held_d, first_d)
        second_d = sums.second(line_d)
        column_c = sums.column(line_c, second_c)
        up_z_c = sums.along_z(column_c)
        column_d = sums.column(line_d, second_d)
        up_z_d = sums.along_z(column_d)
        ffn_block = jnp.concatenate(
            [
                sums.result(column_a, later(up_z_a, give_d)),
                sums.result(column_b, later(up_z_b, give_d)),
            ],
            1,
        )
        block_c, block_d = sums.result(column_c, up_z_c), sums.result(column_d, up_z_d)
        attn_block = jnp.concatenate([block_c[:attn_rows], block_d[:attn_rows]], 1)
        early_vec = block_c[attn_rows:].reshape(-1)[: 10 * D].reshape(10, D)
        late_vec = block_d[attn_rows:].reshape(-1)[: 2 * D].reshape(2, D)
        by_row = ffn_block.reshape(UP_CHUNKS, up_rows, D).transpose(1, 0, 2).reshape(ffn_rows, D)
        ffn_block = jnp.where(holds_up, by_row, ffn_block)
        ffn_summed = to_flat(places, me, ffn_block, early_vec[3:], FFN_TAIL)
        attn_tail = jnp.concatenate([late_vec, early_vec[:3]], 0)
        attn_summed = to_flat(places, me, attn_block, attn_tail, ATTN_TAIL)
    else:
        backs = [back(i, []) for i in range(ATTEND_CALLS)]
        grads = [b[0] for b in backs]
        token_grad = token_gradient(grad_resid, attn_whole, grads, [])
        grads = jnp.concatenate(grads, 2)
        mats = [contract_rows(tokens, grads[i]) for i in range(3)]
        mats.append(contract_rows(jnp.concatenate(mixed, 1), grad_attn_out))
        vectors = jnp.concatenate([b[1] for b in backs], 1)[:2]
        vec_grad = jnp.concatenate([vectors, vec_grad[2:]], 0)
        attn_full = jnp.concatenate([g.reshape(-1) for g in mats + [vec_grad[:5]]])
        up = contract_rows(hidden_low, grad_pre)
        down = contract_rows(activated, grad_ffn_out)
        ffn_full = jnp.concatenate([g.reshape(-1) for g in (up, down, vec_grad[5:12])])
        attn_summed = lax.psum_scatter(attn_full, AXES, scatter_dimension=0, tiled=True)
        ffn_summed = lax.psum_scatter(ffn_full, AXES, scatter_dimension=0, tiled=True)
    attn_grad = attn_summed / token_total
    ffn_grad = ffn_summed / token_total
    attn_change, moment_attn, square_attn, drift_attn = adam_update(
        attn_param, attn_grad, attn_moment, attn_square, attn_shadow
    )
    ffn_change, moment_ffn, square_ffn, drift_ffn = adam_update(
        ffn_param, ffn_grad, ffn_moment, ffn_square, ffn_shadow
    )
    return (
        final_low,
        pooled,
        token_grad,
        attn_grad,
        ffn_grad,
        attn_change,
        ffn_change,
        moment_attn,
        moment_ffn,
        square_attn,
        square_ffn,
        drift_attn,
        drift_ffn,
    )


def solution(mesh):
    rows, flat = P(AXES, None), P(AXES)
    return jax.shard_map(
        functools.partial(on_device, Places(mesh)),
        mesh=mesh,
        in_specs=(rows, flat, flat, rows) + (flat,) * 8,
        out_specs=(rows, rows, rows) + (flat,) * 10,
        check_vma=False,
    )
```

time: 826 us -> 369 us (0.45)
  Pallas kernels: 533 us -> 145 us
  waiting for transfers between devices: 141 us -> 91.5 us
  matrix products: 26.3 us -> 0 us
  starting transfers between devices: 68.8 us -> 60.2 us
    pallas_call x6 -> x13, Pallas kernels: 533 us -> 145 us  [the longest x1 40.5 us: middle(): pl.pallas_call(functools.partial(middle_kernel, fetch, len(sources)), gri...]
    ppermute x52 -> x45, waiting for transfers between devices: 140 us -> 90.1 us  [send(): return lax.ppermute(array, AXES, self.rotation(axis, step))]
    dot_general x12 -> x0, matrix products: 26.3 us -> none  [dot(): lax.dot_general(left, right, (((left_dim,), (right_dim,)), ((), ())), pre...]
    convert_element_type x10 -> x15, other arithmetic: 1.75 us -> 13 us  [the longest x4 9.18 us: held(): return self.add(keep, arrived).astype(BF)]
    unnamed x77 -> x112, local copies, waits for them, and re-layouts: 8.9 us -> 19.4 us
    ppermute x52 -> x45, starting transfers between devices: 56.2 us -> 46.2 us  [send(): return lax.ppermute(array, AXES, self.rotation(axis, step))]
  transfers between devices with their start and end apart: 56 -> 49, of which waited for: 24 -> 21; matrix products, arithmetic and copies ran while one was open for 6% -> 9% of each run, Pallas kernels for 21% -> 22%
where the time goes in v2:
time: 369 us; the launch traced here: 362 us
  Pallas kernels  145 us (39%)
  waiting for transfers between devices  91.5 us (25%)
  starting transfers between devices  60.2 us (16%)
  local copies, waits for them, and re-layouts  30.7 us (8%)
  other arithmetic  29.1 us (8%)
  between operations  5.57 us (2%)
    ppermute x45, waiting for transfers between devices, send(): return lax.ppermute(array, AXES, self.rotation(axis, step))  90.1 us
    ppermute x45, starting transfers between devices, send(): return lax.ppermute(array, AXES, self.rotation(axis, step))  46.2 us
    pallas_call x1, Pallas kernels, middle(): pl.pallas_call(functools.partial(middle_kernel, fetch, len(sources)), gri...  40.5 us
    pallas_call x3, Pallas kernels, attend_back(): pl.pallas_call(attend_back_kernel, grid=(pairs,), in_specs=attend_specs()...  34.6 us
    pallas_call x3, Pallas kernels, attend(): pl.pallas_call(attend_kernel, grid=(pairs,), in_specs=attend_specs() + [p...  26.1 us
    pallas_call x2, Pallas kernels, ffn_terms(): pl.pallas_call(kernel, grid=(2 * UP_CHUNKS,), in_specs=[pl.BlockSpec(memo...  19.9 us
    unnamed x112, local copies, waits for them, and re-layouts  19.4 us
    pallas_call x2, Pallas kernels, attn_terms(): pl.pallas_call(kernel, grid=(4,), in_specs=[pl.BlockSpec(memory_space=plt...  10.8 us
  transfers between devices with their start and end apart: 49, of which 21 were waited for; matrix products, arithmetic and copies ran while one was open for 9% of the time, Pallas kernels for 22%

profile of v2, /device:TPU:8, one launch (start us, length us, event | category | flops | bytes accessed | tf_op | source)
XLA Modules:
  0.0 362.0 jit_solution(14189152813462235773)
XLA Ops:
  1.4 3.4 collective-permute-start
  16.6 8.3 %collective-permute-done.2 = bf16[112,768]{1,0:T(8,128)(2,1)S(1)} collective-permute-done((bf16[112,768]{1,0:T(8,128)(2,1)S(1)}, bf16[112,768]{1,0:T(8,128)(2,1)S(1)}, u32[]{:S(2)}, u32[]{:S(2)}) %collective-permute-start.2) | collective-permute-done | bytes 172064 | tf_op jit(solution)/shard_map/ppermute | solution.py:79
  24.9 3.3 collective-permute-done.3
  29.2 3.9 %collective-permute-start.8 = (bf16[5376]{0:T(1024)(128)(2,1)S(1)}, bf16[5376]{0:T(1024)(128)(2,1)S(1)}, u32[]{:S(2)}, u32[]{:S(2)}) collective-permute-start(bf16[5376]{0:T(1024)(128)(2,1)S(1)} %slice.121), channel_id=1, source_target_pairs={{0,1},{1,2},{2,3},{3,4},{4,5},{5,6},{6,7},{7,8},{8,9},{9,10},{10,1... | collective-permute-start | bytes 32264 | tf_op jit(solution)/shard_map/ppermute | solution.py:204
  33.1 6.6 %collective-permute-done.4 = bf16[400,768]{1,0:T(8,128)(2,1)S(1)} collective-permute-done((bf16[400,768]{1,0:T(8,128)(2,1)}, bf16[400,768]{1,0:T(8,128)(2,1)S(1)}, u32[]{:S(2)}, u32[]{:S(2)}) %collective-permute-start.4) | collective-permute-done | bytes 614432 | tf_op jit(solution)/shard_map/ppermute | solution.py:79
  46.0 4.0 %collective-permute-done.12 = bf16[96,768]{1,0:T(8,128)(2,1)S(1)} collective-permute-done((bf16[96,768]{1,0:T(8,128)(2,1)S(1)}, bf16[96,768]{1,0:T(8,128)(2,1)S(1)}, u32[]{:S(2)}, u32[]{:S(2)}) %collective-permute-start.12) | collective-permute-done | bytes 147488 | tf_op jit(solution)/shard_map/ppermute | solution.py:79
  51.2 6.0 %collective-permute-done.13 = bf16[96,768]{1,0:T(8,128)(2,1)S(1)} collective-permute-done((bf16[96,768]{1,0:T(8,128)(2,1)S(1)}, bf16[96,768]{1,0:T(8,128)(2,1)S(1)}, u32[]{:S(2)}, u32[]{:S(2)}) %collective-permute-start.13) | collective-permute-done | bytes 147488 | tf_op jit(solution)/shard_map/ppermute | solution.py:79
  57.8 4.3 %collective-permute-done.14 = bf16[96,768]{1,0:T(8,128)(2,1)S(1)} collective-permute-done((bf16[96,768]{1,0:T(8,128)(2,1)S(1)}, bf16[96,768]{1,0:T(8,128)(2,1)S(1)}, u32[]{:S(2)}, u32[]{:S(2)}) %collective-permute-start.14) | collective-permute-done | bytes 147488 | tf_op jit(solution)/shard_map/ppermute | solution.py:79
  63.0 4.7 %collective-permute-done.11 = bf16[96,768]{1,0:T(8,128)(2,1)S(1)} collective-permute-done((bf16[96,768]{1,0:T(8,128)(2,1)S(1)}, bf16[96,768]{1,0:T(8,128)(2,1)S(1)}, u32[]{:S(2)}, u32[]{:S(2)}) %collective-permute-start.11) | collective-permute-done | bytes 147488 | tf_op jit(solution)/shard_map/ppermute | solution.py:79
  69.0 3.6 %collective-permute-done.16 = bf16[384,768]{1,0:T(8,128)(2,1)} collective-permute-done((bf16[384,768]{1,0:T(8,128)(2,1)S(1)}, bf16[384,768]{1,0:T(8,128)(2,1)}, u32[]{:S(2)}, u32[]{:S(2)}) %collective-permute-start.16) | collective-permute-done | bytes 589856 | tf_op jit(solution)/shard_map/ppermute | solution.py:79
  73.8 5.2 %collective-permute-done.15 = bf16[384,768]{1,0:T(8,128)(2,1)} collective-permute-done((bf16[384,768]{1,0:T(8,128)(2,1)S(1)}, bf16[384,768]{1,0:T(8,128)(2,1)}, u32[]{:S(2)}, u32[]{:S(2)}) %collective-permute-start.15) | collective-permute-done | bytes 589856 | tf_op jit(solution)/shard_map/ppermute | solution.py:79
  80.1 7.6 %project.1 = (bf16[1024,768]{1,0:T(8,128)(2,1)S(1)}, bf16[1024,768]{1,0:T(8,128)(2,1)S(1)}, bf16[1024,768]{1,0:T(8,128)(2,1)S(1)}, f32[16,768]{1,0:T(8,128)S(1)}, bf16[3072,768]{1,0:T(8,128)(2,1)S(1)}) custom-call(s32[4]{0:T(128)S(1)} %pad_add_fusion.me.me_ref, bf16[1024,768]{1,0:T(8,128)(2,1)S(1)} %copy-done.8, ...), custom_call_target="tpu_custom_call" | custom-call | flops 8800000000 | bytes 1048576 | tf_op jit(solution)/shard_map/project/pallas_call | solution.py:268
  92.0 8.6 %attend.5 = (bf16[1024,256]{1,0:T(8,128)(2,1)S(1)}, f32[2,8,1024]{2,1,0:T(8,128)S(1)}) custom-call(s32[1]{0:T(128)} %copy.93.count, s32[1024,1]{1,0:T(8,128)S(1)} %copy.51.seg_column, s32[1,1024]{1,0:T(1,128)S(1)} %bitcast.163, bf16[1024,768]{1,0:T(8,128)(2,1)S(1)} %get-tuple-element.72.query, bf16[1024,768]{1,0:T(8,128)(2,1)S(1)} %get-tuple-element.73.key, ...), custom_call_target="tpu_custom_call" | custom-call | flops 9166666752 | bytes 1048576 | tf_op jit(solution)/shard_map/attend/pallas_call | solution.py:371
  100.6 8.6 %attend.4 = (bf16[1024,256]{1,0:T(8,128)(2,1)S(1)}, f32[2,8,1024]{2,1,0:T(8,128)S(1)}) custom-call(s32[1]{0:T(128)} %copy.93.count, s32[1024,1]{1,0:T(8,128)S(1)} %copy.51.seg_column, s32[1,1024]{1,0:T(1,128)S(1)} %bitcast.164, bf16[1024,768]{1,0:T(8,128)(2,1)S(1)} %get-tuple-element.72.query, bf16[1024,768]{1,0:T(8,128)(2,1)S(1)} %get-tuple-element.73.key, ...), custom_call_target="tpu_custom_call" | custom-call | flops 9166666752 | bytes 1048576 | tf_op jit(solution)/shard_map/attend/pallas_call | solution.py:371
  109.4 9.4 %collective-permute-done.17 = bf16[768,768]{1,0:T(8,128)(2,1)S(1)} collective-permute-done((bf16[768,768]{1,0:T(8,128)(2,1)S(1)}, bf16[768,768]{1,0:T(8,128)(2,1)S(1)}, u32[]{:S(2)}, u32[]{:S(2)}) %collective-permute-start.17) | collective-permute-done | bytes 1179680 | tf_op jit(solution)/shard_map/ppermute | solution.py:79
  118.8 8.8 %attend.3 = (bf16[1024,256]{1,0:T(8,128)(2,1)S(1)}, f32[2,8,1024]{2,1,0:T(8,128)S(1)}) custom-call(s32[1]{0:T(128)} %copy.93.count, s32[1024,1]{1,0:T(8,128)S(1)} %copy.51.seg_column, s32[1,1024]{1,0:T(1,128)S(1)} %bitcast.165, bf16[1024,768]{1,0:T(8,128)(2,1)S(1)} %get-tuple-element.72.query, bf16[1024,768]{1,0:T(8,128)(2,1)S(1)} %get-tuple-element.73.key, ...), custom_call_target="tpu_custom_call" | custom-call | flops 9166666752 | bytes 1048576 | tf_op jit(solution)/shard_map/attend/pallas_call | solution.py:371
  128.8 40.5 %middle.1 = (bf16[1024,768]{1,0:T(8,128)(2,1)}, bf16[1024,768]{1,0:T(8,128)(2,1)}, bf16[1024,3072]{1,0:T(8,128)(2,1)}, bf16[1024,3072]{1,0:T(8,128)(2,1)}, bf16[...) custom-call(s32[1]{0:T(128)} %copy.93.count, ...), custom_call_target="tpu_custom_call" | custom-call | flops 44000002048 | bytes 1048576 | tf_op jit(solution)/shard_map/middle/pallas_call | solution.py:612
  177.6 11.5 %ffn_terms.2 = (bf16[2,8,192,512]{3,2,1,0:T(8,128)(2,1)S(1)}, bf16[2,8,192,512]{3,2,1,0:T(8,128)(2,1)}) custom-call(s32[4]{0:T(128)S(1)} %pad_add_fusion.me.me_ref, bf16[1024,768]{1,0:T(8,128)(2,1)S(1)} %copy-done.13, bf16[1024,3072]{1,0:T(8,128)(2,1)S(1)} %copy-done.11, bf16[1024,3072]{1,0:T(8,128)(2,1)S(1)} %copy-done.12, ...), custom_call_target="tpu_custom_call" | custom-call | flops 11000000512 | bytes 1048576 | tf_op jit(solution)/shard_map/ffn_terms/pallas_call | solution.py:729
  189.2 8.4 %ffn_terms.3 = (bf16[2,8,192,256]{3,2,1,0:T(8,128)(2,1)S(1)}, bf16[2,8,192,256]{3,2,1,0:T(8,128)(2,1)}) custom-call(s32[4]{0:T(128)S(1)} %pad_add_fusion.me.me_ref, bf16[1024,768]{1,0:T(8,128)(2,1)S(1)} %copy-done.13, bf16[1024,3072]{1,0:T(8,128)(2,1)S(1)} %copy-done.11, bf16[1024,3072]{1,0:T(8,128)(2,1)S(1)} %copy-done.12, ...), custom_call_target="tpu_custom_call" | custom-call | flops 5500000256 | bytes 1048576 | tf_op jit(solution)/shard_map/ffn_terms/pallas_call | solution.py:729
  211.5 11.3 %attend_back.3 = (bf16[3,1024,256]{2,1,0:T(8,128)(2,1)S(1)}, f32[8,256]{1,0:T(8,128)S(1)}) custom-call(s32[1]{0:T(128)} %copy.93.count, s32[1024,1]{1,0:T(8,128)S(1)} %copy-done.6, s32[1,1024]{1,0:T(1,128)S(1)} %bitcast.167, bf16[1024,768]{1,0:T(8,128)(2,1)S(1)} %copy-done.36, bf16[1024,768]{1,0:T(8,128)(2,1)S(1)} %copy-done.38, ...), custom_call_target="tpu_custom_call" | custom-call | flops 12099999744 | bytes 1048576 | tf_op jit(solution)/shard_map/attend_back/pallas_call | solution.py:430
  222.8 14.7 %collective-permute-done.26 = bf16[4,2,192,256]{3,2,0,1:T(8,128)(2,1)S(1)} collective-permute-done((bf16[4,2,192,256]{3,2,0,1:T(8,128)(2,1)S(1)}, bf16[4,2,192,256]{3,2,0,1:T(8,128)(2,1)S(1)}, u32[]{:S(2)}, u32[]{:S(2)}) %collective-permute-start.26) | collective-permute-done | bytes 786464 | tf_op jit(solution)/shard_map/ppermute | solution.py:79
  241.1 11.7 %attend_back.4 = (bf16[3,1024,256]{2,1,0:T(8,128)(2,1)S(1)}, f32[8,256]{1,0:T(8,128)S(1)}) custom-call(s32[1]{0:T(128)} %copy.93.count, s32[1024,1]{1,0:T(8,128)S(1)} %copy-done.6, s32[1,1024]{1,0:T(1,128)S(1)} %bitcast.168, bf16[1024,768]{1,0:T(8,128)(2,1)S(1)} %copy-done.36, bf16[1024,768]{1,0:T(8,128)(2,1)S(1)} %copy-done.38, ...), custom_call_target="tpu_custom_call" | custom-call | flops 12099999744 | bytes 1048576 | tf_op jit(solution)/shard_map/attend_back/pallas_call | solution.py:430
  255.3 6.3 %attn_terms.2 = (bf16[2,8,112,512]{3,2,1,0:T(8,128)(2,1)S(1)}, bf16[2,8,112,512]{3,2,1,0:T(8,128)(2,1)}) custom-call(s32[4]{0:T(128)S(1)} %pad_add_fusion.me.me_ref, bf16[1024,768]{1,0:T(8,128)(2,1)S(1)} %copy-done.9, bf16[16,512]{1,0:T(8,128)(2,1)S(1)} %reshape.188.vectors_ref, bf16[1024,256]{1,0:T(8,128)(2,1)S(1)} %copy-done.28, ...), custom_call_target="tpu_custom_call" | custom-call | flops 4400000000 | bytes 1048576 | tf_op jit(solution)/shard_map/attn_terms/pallas_call | solution.py:813
  267.1 11.5 %attend_back.5 = (bf16[3,1024,256]{2,1,0:T(8,128)(2,1)S(1)}, f32[8,256]{1,0:T(8,128)S(1)}) custom-call(s32[1]{0:T(128)} %copy.93.count, s32[1024,1]{1,0:T(8,128)S(1)} %copy-done.6, s32[1,1024]{1,0:T(1,128)S(1)} %bitcast.169, bf16[1024,768]{1,0:T(8,128)(2,1)S(1)} %copy-done.36, bf16[1024,768]{1,0:T(8,128)(2,1)S(1)} %copy-done.38, ...), custom_call_target="tpu_custom_call" | custom-call | flops 12099999744 | bytes 1048576 | tf_op jit(solution)/shard_map/attend_back/pallas_call | solution.py:430
  281.6 3.7 %collective-permute-start.43 = (bf16[192,512]{1,0:T(8,128)(2,1)S(1)}, bf16[192,512]{1,0:T(8,128)(2,1)S(1)}, u32[]{:S(2)}, u32[]{:S(2)}) collective-permute-start(bf16[192,512]{1,0:T(8,128)(2,1)S(1)} %get-tuple-element.151), channel_id=1, source_target_pairs={{0,4},{1,5},{2,6},{3,7},{4,0},{5,1},{6,2},{7,3},{8,12},{9,13},{10,... | collective-permute-start | bytes 589832 | tf_op jit(solution)/shard_map/ppermute | solution.py:79
  292.6 5.6 %collective-permute-done.43 = bf16[192,512]{1,0:T(8,128)(2,1)S(1)} collective-permute-done((bf16[192,512]{1,0:T(8,128)(2,1)S(1)}, bf16[192,512]{1,0:T(8,128)(2,1)S(1)}, u32[]{:S(2)}, u32[]{:S(2)}) %collective-permute-start.43) | collective-permute-done | bytes 196640 | tf_op jit(solution)/shard_map/ppermute | solution.py:79
  300.2 4.5 %attn_terms.3 = (bf16[2,8,112,256]{3,2,1,0:T(8,128)(2,1)S(1)}, bf16[2,8,112,256]{3,2,1,0:T(8,128)(2,1)}) custom-call(s32[4]{0:T(128)S(1)} %pad_add_fusion.me.me_ref, bf16[1024,768]{1,0:T(8,128)(2,1)S(1)} %copy-done.10, bf16[16,256]{1,0:T(8,128)(2,1)S(1)} %reshape.190.vectors_ref, bf16[1024,256]{1,0:T(8,128)(2,1)S(1)} %copy-done.29, ...), custom_call_target="tpu_custom_call" | custom-call | flops 2750000128 | bytes 1048576 | tf_op jit(solution)/shard_map/attn_terms/pallas_call | solution.py:813
  311.7 3.0 collective-permute-start.48
  321.2 5.6 %token_grad.1 = bf16[1024,768]{1,0:T(8,128)(2,1)} custom-call(f32[1024,768]{1,0:T(8,128)S(1)} %copy-done.30, bf16[3072,768]{1,0:T(8,128)(2,1)S(1)} %bitcast.176, bf16[3,1024,256]{2,1,0:T(8,128)(2,1)S(1)} %copy-done.32, bf16[3,1024,256]{2,1,0:T(8,128)(2,1)S(1)} %copy-done.34, bf16[3,1024,256]{2,1,0:T(8,128)(2,1)S(1)} %copy-done.19, ...), custom_call_target="tpu_custom_call" | custom-call | flops 5500000256 | bytes 1048576 | tf_op jit(solution)/shard_map/token_grad/pallas_call | solution.py:853
  329.5 5.1 %collective-permute-start.33 = (bf16[112,512]{1,0:T(8,128)(2,1)S(1)}, bf16[112,512]{1,0:T(8,128)(2,1)S(1)}, u32[]{:S(2)}, u32[]{:S(2)}) collective-permute-start(bf16[112,512]{1,0:T(8,128)(2,1)S(1)} %get-tuple-element.154), channel_id=1, source_target_pairs={{0,4},{1,5},{2,6},{3,7},{4,0},{5,1},{6,2},{7,3},{8,12},{9,13},{10,... | collective-permute-start | bytes 344072 | tf_op jit(solution)/shard_map/ppermute | solution.py:79
  351.9 3.8 %collective-permute-start.41 = (f32[5,768]{1,0:T(8,128)S(1)}, f32[5,768]{1,0:T(8,128)S(1)}, u32[]{:S(2)}, u32[]{:S(2)}) collective-permute-start(f32[5,768]{1,0:T(8,128)S(1)} %pad_maximum_fusion.7), channel_id=1, source_target_pairs={{1,0},{2,1},{3,2},{4,3},{5,4},{6,5},{7,6},{8,7},{9,8},{10,9},{11,1... | collective-permute-start | bytes 46088 | tf_op jit(solution)/shard_map/ppermute | solution.py:212
  355.7 3.5 subtract_multiply_fusion
  (309 shorter events, 109.3 us)
Async XLA Ops:
  10.9 14.0 %collective-permute-start.2 = (bf16[112,768]{1,0:T(8,128)(2,1)S(1)}, bf16[112,768]{1,0:T(8,128)(2,1)S(1)}, u32[]{:S(2)}, u32[]{:S(2)}) collective-permute-start(bf16[112,768]{1,0:T(8,128)(2,1)S(1)} %constant_dynamic-update-slice_fusion.9), channel_id=1, source_target_pairs={{0,4},{1,5},{2,6},{3,7},{4,0},{5,1},{6,2},{7,3},{8,12},{9,13},{10,... | collective-permute-start | bytes 516104 | tf_op jit(solution)/shard_map/ppermute | solution.py:79
  12.0 16.1 %collective-permute-start.3 = (bf16[112,768]{1,0:T(8,128)(2,1)S(1)}, bf16[112,768]{1,0:T(8,128)(2,1)S(1)}, u32[]{:S(2)}, u32[]{:S(2)}) collective-permute-start(bf16[112,768]{1,0:T(8,128)(2,1)S(1)} %constant_dynamic-update-slice_fusion.9), channel_id=1, source_target_pairs={{0,6},{1,7},{2,0},{3,1},{4,2},{5,3},{6,4},{7,5},{8,14},{9,15},{10,... | collective-permute-start | bytes 516104 | tf_op jit(solution)/shard_map/ppermute | solution.py:79
  29.2 12.3 %collective-permute-start.8 = (bf16[5376]{0:T(1024)(128)(2,1)S(1)}, bf16[5376]{0:T(1024)(128)(2,1)S(1)}, u32[]{:S(2)}, u32[]{:S(2)}) collective-permute-start(bf16[5376]{0:T(1024)(128)(2,1)S(1)} %slice.121), channel_id=1, source_target_pairs={{0,1},{1,2},{2,3},{3,4},{4,5},{5,6},{6,7},{7,8},{8,9},{9,10},{10,1... | collective-permute-start | bytes 32264 | tf_op jit(solution)/shard_map/ppermute | solution.py:204
  39.9 17.4 %collective-permute-start.5 = (bf16[784,768]{1,0:T(8,128)(2,1)S(1)}, bf16[784,768]{1,0:T(8,128)(2,1)}, u32[]{:S(2)}, u32[]{:S(2)}) collective-permute-start(bf16[784,768]{1,0:T(8,128)(2,1)S(1)} %pad_maximum_fusion.refs_0_), channel_id=1, source_target_pairs={{0,16},{1,17},{2,18},{3,19},{4,20},{5,21},{6,22},{7,23},{8,9},{9,8... | collective-permute-start | bytes 3612680 | tf_op jit(solution)/shard_map/ppermute | solution.py:79
  42.4 14.8 %collective-permute-start.13 = (bf16[96,768]{1,0:T(8,128)(2,1)S(1)}, bf16[96,768]{1,0:T(8,128)(2,1)S(1)}, u32[]{:S(2)}, u32[]{:S(2)}) collective-permute-start(bf16[96,768]{1,0:T(8,128)(2,1)S(1)} %get-tuple-element.160), channel_id=1, source_target_pairs={{0,4},{1,5},{2,6},{3,7},{4,0},{5,1},{6,2},{7,3},{8,12},{9,13},{10,... | collective-permute-start | bytes 442376 | tf_op jit(solution)/shard_map/ppermute | solution.py:79
  43.3 18.7 %collective-permute-start.14 = (bf16[96,768]{1,0:T(8,128)(2,1)S(1)}, bf16[96,768]{1,0:T(8,128)(2,1)S(1)}, u32[]{:S(2)}, u32[]{:S(2)}) collective-permute-start(bf16[96,768]{1,0:T(8,128)(2,1)S(1)} %get-tuple-element.160), channel_id=1, source_target_pairs={{0,6},{1,7},{2,0},{3,1},{4,2},{5,3},{6,4},{7,5},{8,14},{9,15},{10,... | collective-permute-start | bytes 442376 | tf_op jit(solution)/shard_map/ppermute | solution.py:79
  44.6 18.0 %collective-permute-start.9 = (bf16[96,768]{1,0:T(8,128)(2,1)S(1)}, bf16[96,768]{1,0:T(8,128)(2,1)S(1)}, u32[]{:S(2)}, u32[]{:S(2)}) collective-permute-start(bf16[96,768]{1,0:T(8,128)(2,1)S(1)} %get-tuple-element.162), channel_id=1, source_target_pairs={{0,2},{1,3},{2,4},{3,5},{4,6},{5,7},{6,0},{7,1},{8,10},{9,11},{10,... | collective-permute-start | bytes 442376 | tf_op jit(solution)/shard_map/ppermute | solution.py:79
  50.0 12.9 %collective-permute-start.10 = (bf16[96,768]{1,0:T(8,128)(2,1)S(1)}, bf16[96,768]{1,0:T(8,128)(2,1)S(1)}, u32[]{:S(2)}, u32[]{:S(2)}) collective-permute-start(bf16[96,768]{1,0:T(8,128)(2,1)S(1)} %get-tuple-element.162), channel_id=1, source_target_pairs={{0,4},{1,5},{2,6},{3,7},{4,0},{5,1},{6,2},{7,3},{8,12},{9,13},{10,... | collective-permute-start | bytes 442376 | tf_op jit(solution)/shard_map/ppermute | solution.py:79
  57.2 22.9 %collective-permute-start.6 = (bf16[784,768]{1,0:T(8,128)(2,1)S(1)}, bf16[784,768]{1,0:T(8,128)(2,1)}, u32[]{:S(2)}, u32[]{:S(2)}) collective-permute-start(bf16[784,768]{1,0:T(8,128)(2,1)S(1)} %pad_maximum_fusion.refs_0_), channel_id=1, source_target_pairs={{0,8},{1,9},{2,10},{3,11},{4,12},{5,13},{6,14},{7,15},{8,0},{9,1},... | collective-permute-start | bytes 3612680 | tf_op jit(solution)/shard_map/ppermute | solution.py:79
  57.2 22.9 %collective-permute-start.7 = (bf16[784,768]{1,0:T(8,128)(2,1)}, bf16[784,768]{1,0:T(8,128)(2,1)}, u32[]{:S(2)}, u32[]{:S(2)}) collective-permute-start(bf16[784,768]{1,0:T(8,128)(2,1)} %collective-permute-done.5.refs_1_), channel_id=1, source_target_pairs={{0,8},{1,9},{2,10},{3,11},{4,12},{5,13},{6,14},{7,15},{8,0},{9,1},... | collective-permute-start | bytes 3612680 | tf_op jit(solution)/shard_map/ppermute | solution.py:79
  67.7 11.3 %collective-permute-start.15 = (bf16[384,768]{1,0:T(8,128)(2,1)S(1)}, bf16[384,768]{1,0:T(8,128)(2,1)}, u32[]{:S(2)}, u32[]{:S(2)}) collective-permute-start(bf16[384,768]{1,0:T(8,128)(2,1)S(1)} %constant_dynamic-update-slice_fusion.4.refs_4_), channel_id=1, source_target_pairs={{0,1},{1,0},{2,3},{3,2},{4,5},{5,4},{6,7},{7,6},{8,24},{9,25},{10,... | collective-permute-start | bytes 1769480 | tf_op jit(solution)/shard_map/ppermute | solution.py:79
  89.9 37.8 %collective-permute-start.21 = (bf16[768,768]{1,0:T(8,128)(2,1)S(1)}, bf16[768,768]{1,0:T(8,128)(2,1)S(1)}, u32[]{:S(2)}, u32[]{:S(2)}) collective-permute-start(bf16[768,768]{1,0:T(8,128)(2,1)S(1)} %pad_maximum_fusion.2.refs_0_), channel_id=1, source_target_pairs={{0,8},{1,9},{2,10},{3,11},{4,12},{5,13},{6,14},{7,15},{8,0},{9,1},... | collective-permute-start | bytes 3538952 | tf_op jit(solution)/shard_map/ppermute | solution.py:79
  89.9 19.4 %collective-permute-start.20 = (bf16[768,768]{1,0:T(8,128)(2,1)S(1)}, bf16[768,768]{1,0:T(8,128)(2,1)S(1)}, u32[]{:S(2)}, u32[]{:S(2)}) collective-permute-start(bf16[768,768]{1,0:T(8,128)(2,1)S(1)} %pad_maximum_fusion.2.refs_0_), channel_id=1, source_target_pairs={{0,16},{1,17},{2,18},{3,19},{4,20},{5,21},{6,22},{7,23},{8,9},{9,8... | collective-permute-start | bytes 3538952 | tf_op jit(solution)/shard_map/ppermute | solution.py:79
  90.2 37.5 %collective-permute-start.18 = (bf16[768,768]{1,0:T(8,128)(2,1)S(1)}, bf16[768,768]{1,0:T(8,128)(2,1)S(1)}, u32[]{:S(2)}, u32[]{:S(2)}) collective-permute-start(bf16[768,768]{1,0:T(8,128)(2,1)S(1)} %pad_maximum_fusion.1.refs_0_), channel_id=1, source_target_pairs={{0,8},{1,9},{2,10},{3,11},{4,12},{5,13},{6,14},{7,15},{8,0},{9,1},... | collective-permute-start | bytes 3538952 | tf_op jit(solution)/shard_map/ppermute | solution.py:79
  90.4 28.4 %collective-permute-start.17 = (bf16[768,768]{1,0:T(8,128)(2,1)S(1)}, bf16[768,768]{1,0:T(8,128)(2,1)S(1)}, u32[]{:S(2)}, u32[]{:S(2)}) collective-permute-start(bf16[768,768]{1,0:T(8,128)(2,1)S(1)} %pad_maximum_fusion.1.refs_0_), channel_id=1, source_target_pairs={{0,16},{1,17},{2,18},{3,19},{4,20},{5,21},{6,22},{7,23},{8,9},{9,8... | collective-permute-start | bytes 3538952 | tf_op jit(solution)/shard_map/ppermute | solution.py:79
  109.3 18.4 %collective-permute-start.22 = (bf16[768,768]{1,0:T(8,128)(2,1)S(1)}, bf16[768,768]{1,0:T(8,128)(2,1)S(1)}, u32[]{:S(2)}, u32[]{:S(2)}) collective-permute-start(bf16[768,768]{1,0:T(8,128)(2,1)S(1)} %collective-permute-done.20), channel_id=1, source_target_pairs={{0,8},{1,9},{2,10},{3,11},{4,12},{5,13},{6,14},{7,15},{8,0},{9,1},... | collective-permute-start | bytes 3538952 | tf_op jit(solution)/shard_map/ppermute | solution.py:79
  189.1 13.9 %collective-permute-start.23 = (bf16[2,4,2,192,512]{4,3,2,1,0:T(8,128)(2,1)}, bf16[2,4,2,192,512]{4,3,2,1,0:T(8,128)(2,1)}, u32[]{:S(2)}, u32[]{:S(2)}) collective-permute-start(bf16[2,4,2,192,512]{4,3,2,1,0:T(8,128)(2,1)} %bitcast.22.refs_2_), channel_id=1, source_target_pairs={{0,8},{1,9},{2,10},{3,11},{4,12},{5,13},{6,14},{7,15},{8,0},{9,1},... | collective-permute-start | bytes 9437192 | tf_op jit(solution)/shard_map/ppermute | solution.py:79
  208.6 29.7 %collective-permute-start.25 = (bf16[4,2,192,512]{3,2,0,1:T(8,128)(2,1)S(1)}, bf16[4,2,192,512]{3,2,0,1:T(8,128)(2,1)S(1)}, u32[]{:S(2)}, u32[]{:S(2)}) collective-permute-start(bf16[4,2,192,512]{3,2,0,1:T(8,128)(2,1)S(1)} %bitcast_select_fusion), channel_id=1, source_target_pairs={{0,1},{1,0},{2,3},{3,2},{4,5},{5,4},{6,7},{7,6},{8,24},{9,25},{10,... | collective-permute-start | bytes 4718600 | tf_op jit(solution)/shard_map/ppermute | solution.py:79
  209.1 28.5 %collective-permute-start.26 = (bf16[4,2,192,256]{3,2,0,1:T(8,128)(2,1)S(1)}, bf16[4,2,192,256]{3,2,0,1:T(8,128)(2,1)S(1)}, u32[]{:S(2)}, u32[]{:S(2)}) collective-permute-start(bf16[4,2,192,256]{3,2,0,1:T(8,128)(2,1)S(1)} %bitcast_select_fusion.4), channel_id=1, source_target_pairs={{0,1},{1,0},{2,3},{3,2},{4,5},{5,4},{6,7},{7,6},{8,24},{9,25},{10,... | collective-permute-start | bytes 2359304 | tf_op jit(solution)/shard_map/ppermute | solution.py:79
  238.0 14.8 %collective-permute-start.28 = (bf16[4,192,256]{2,1,0:T(8,128)(2,1)S(1)}, bf16[4,192,256]{2,1,0:T(8,128)(2,1)S(1)}, u32[]{:S(2)}, u32[]{:S(2)}) collective-permute-start(bf16[4,192,256]{2,1,0:T(8,128)(2,1)S(1)} %dynamic-slice_bitcast_fusion.6), channel_id=1, source_target_pairs={{0,16},{1,17},{2,18},{3,19},{4,20},{5,21},{6,22},{7,23},{8,9},{9,8... | collective-permute-start | bytes 1179656 | tf_op jit(solution)/shard_map/ppermute | solution.py:79
  239.2 15.1 %collective-permute-start.27 = (bf16[4,192,512]{2,1,0:T(8,128)(2,1)S(1)}, bf16[4,192,512]{2,1,0:T(8,128)(2,1)S(1)}, u32[]{:S(2)}, u32[]{:S(2)}) collective-permute-start(bf16[4,192,512]{2,1,0:T(8,128)(2,1)S(1)} %dynamic-slice_bitcast_fusion.2), channel_id=1, source_target_pairs={{0,16},{1,17},{2,18},{3,19},{4,20},{5,21},{6,22},{7,23},{8,9},{9,8... | collective-permute-start | bytes 2359304 | tf_op jit(solution)/shard_map/ppermute | solution.py:79
  262.8 18.8 %collective-permute-start.29 = (bf16[2,4,2,112,512]{4,3,2,1,0:T(8,128)(2,1)}, bf16[2,4,2,112,512]{4,3,2,1,0:T(8,128)(2,1)}, u32[]{:S(2)}, u32[]{:S(2)}) collective-permute-start(bf16[2,4,2,112,512]{4,3,2,1,0:T(8,128)(2,1)} %bitcast.41.refs_0_), channel_id=1, source_target_pairs={{0,8},{1,9},{2,10},{3,11},{4,12},{5,13},{6,14},{7,15},{8,0},{9,1},... | collective-permute-start | bytes 5505032 | tf_op jit(solution)/shard_map/ppermute | solution.py:79
  263.6 41.3 %collective-permute-start.45 = (bf16[192,256]{1,0:T(8,128)(2,1)}, bf16[192,256]{1,0:T(8,128)(2,1)S(1)}, u32[]{:S(2)}, u32[]{:S(2)}) collective-permute-start(bf16[192,256]{1,0:T(8,128)(2,1)} %get-tuple-element.155), channel_id=1, source_target_pairs={{0,2},{1,3},{2,4},{3,5},{4,6},{5,7},{6,0},{7,1},{8,10},{9,11},{10,... | collective-permute-start | bytes 294920 | tf_op jit(solution)/shard_map/ppermute | solution.py:79
  265.6 39.3 %collective-permute-start.46 = (bf16[192,256]{1,0:T(8,128)(2,1)}, bf16[192,256]{1,0:T(8,128)(2,1)}, u32[]{:S(2)}, u32[]{:S(2)}) collective-permute-start(bf16[192,256]{1,0:T(8,128)(2,1)} %get-tuple-element.157), channel_id=1, source_target_pairs={{0,4},{1,5},{2,6},{3,7},{4,0},{5,1},{6,2},{7,3},{8,12},{9,13},{10,... | collective-permute-start | bytes 294920 | tf_op jit(solution)/shard_map/ppermute | solution.py:79
  266.6 38.3 %collective-permute-start.47 = (bf16[192,256]{1,0:T(8,128)(2,1)}, bf16[192,256]{1,0:T(8,128)(2,1)}, u32[]{:S(2)}, u32[]{:S(2)}) collective-permute-start(bf16[192,256]{1,0:T(8,128)(2,1)} %get-tuple-element.156), channel_id=1, source_target_pairs={{0,6},{1,7},{2,0},{3,1},{4,2},{5,3},{6,4},{7,5},{8,14},{9,15},{10,... | collective-permute-start | bytes 294920 | tf_op jit(solution)/shard_map/ppermute | solution.py:79
  281.6 16.6 %collective-permute-start.43 = (bf16[192,512]{1,0:T(8,128)(2,1)S(1)}, bf16[192,512]{1,0:T(8,128)(2,1)S(1)}, u32[]{:S(2)}, u32[]{:S(2)}) collective-permute-start(bf16[192,512]{1,0:T(8,128)(2,1)S(1)} %get-tuple-element.151), channel_id=1, source_target_pairs={{0,4},{1,5},{2,6},{3,7},{4,0},{5,1},{6,2},{7,3},{8,12},{9,13},{10,... | collective-permute-start | bytes 589832 | tf_op jit(solution)/shard_map/ppermute | solution.py:79
  290.2 14.6 %collective-permute-start.44 = (bf16[192,512]{1,0:T(8,128)(2,1)S(1)}, bf16[192,512]{1,0:T(8,128)(2,1)S(1)}, u32[]{:S(2)}, u32[]{:S(2)}) collective-permute-start(bf16[192,512]{1,0:T(8,128)(2,1)S(1)} %get-tuple-element.150), channel_id=1, source_target_pairs={{0,6},{1,7},{2,0},{3,1},{4,2},{5,3},{6,4},{7,5},{8,14},{9,15},{10,... | collective-permute-start | bytes 589832 | tf_op jit(solution)/shard_map/ppermute | solution.py:79
  298.2 16.5 %collective-permute-start.30 = (bf16[4,2,112,512]{3,2,0,1:T(8,128)(2,1)}, bf16[4,2,112,512]{3,2,0,1:T(8,128)(2,1)}, u32[]{:S(2)}, u32[]{:S(2)}) collective-permute-start(bf16[4,2,112,512]{3,2,0,1:T(8,128)(2,1)} %bitcast_select_fusion.2), channel_id=1, source_target_pairs={{0,1},{1,0},{2,3},{3,2},{4,5},{5,4},{6,7},{7,6},{8,24},{9,25},{10,... | collective-permute-start | bytes 2752520 | tf_op jit(solution)/shard_map/ppermute | solution.py:79
  304.7 11.9 %collective-permute-start.35 = (bf16[2,4,2,112,256]{4,3,2,1,0:T(8,128)(2,1)}, bf16[2,4,2,112,256]{4,3,2,1,0:T(8,128)(2,1)}, u32[]{:S(2)}, u32[]{:S(2)}) collective-permute-start(bf16[2,4,2,112,256]{4,3,2,1,0:T(8,128)(2,1)} %bitcast.43.refs_3_), channel_id=1, source_target_pairs={{0,8},{1,9},{2,10},{3,11},{4,12},{5,13},{6,14},{7,15},{8,0},{9,1},... | collective-permute-start | bytes 2752520 | tf_op jit(solution)/shard_map/ppermute | solution.py:79
  311.7 30.8 %collective-permute-start.48 = (f32[7,768]{1,0:T(8,128)}, f32[7,768]{1,0:T(8,128)}, u32[]{:S(2)}, u32[]{:S(2)}) collective-permute-start(f32[7,768]{1,0:T(8,128)} %slice.167), channel_id=1, source_target_pairs={{1,0},{2,1},{3,2},{4,3},{5,4},{6,5},{7,6},{8,7},{9,8},{10,9},{11,1... | collective-permute-start | bytes 64520 | tf_op jit(solution)/shard_map/ppermute | solution.py:212
  316.5 11.8 %collective-permute-start.31 = (bf16[4,112,512]{2,1,0:T(8,128)(2,1)S(1)}, bf16[4,112,512]{2,1,0:T(8,128)(2,1)S(1)}, u32[]{:S(2)}, u32[]{:S(2)}) collective-permute-start(bf16[4,112,512]{2,1,0:T(8,128)(2,1)S(1)} %dynamic-slice_bitcast_fusion.5), channel_id=1, source_target_pairs={{0,16},{1,17},{2,18},{3,19},{4,20},{5,21},{6,22},{7,23},{8,9},{9,8... | collective-permute-start | bytes 1376264 | tf_op jit(solution)/shard_map/ppermute | solution.py:79
  318.4 16.3 %collective-permute-start.36 = (bf16[4,2,112,256]{3,2,0,1:T(8,128)(2,1)S(1)}, bf16[4,2,112,256]{3,2,0,1:T(8,128)(2,1)S(1)}, u32[]{:S(2)}, u32[]{:S(2)}) collective-permute-start(bf16[4,2,112,256]{3,2,0,1:T(8,128)(2,1)S(1)} %bitcast_select_fusion.6), channel_id=1, source_target_pairs={{0,1},{1,0},{2,3},{3,2},{4,5},{5,4},{6,7},{7,6},{8,24},{9,25},{10,... | collective-permute-start | bytes 1376264 | tf_op jit(solution)/shard_map/ppermute | solution.py:79
  (73 other events, 673.7 us)
